TPU v7x, 256 devices: a whole 4x4x8 slice. The times are simulated.
256 devices in a mesh: animal: 32 (over z, y), snp: 8 (over x, core).
Axes of the slice: x: 4, y: 4, z: 8, core: 2. Of those that a mesh axis runs over, the one named last changes fastest.
Arguments:
- genotype: bfloat16 [32768, 32768], P('animal', 'snp')
- allele_freq: float32 [32768], P('snp')
- right_side: float32 [32768, 128], P('animal'), may hold values from -6 to 6
- diagonal: float32 [32768, 128], P('animal'), may hold values from 0.5 to 2
- mendelian: float32 [32768], P('animal'), may hold values from 2 to 4
- genomic_weight: float32 [128], replicated, may hold values from 1 to 8
- send_rows: int32 [32, 32, 64], P('animal'), may hold values from 0 to 1023, as said below
- sire_slot: int32 [32768], P('animal'), may hold values from 0 to 1999, as said below
- dam_slot: int32 [32768], P('animal'), may hold values from 16 to 2047, as said below
Outputs:
- solution: float32 [32768, 128], P('animal')
- residual: float32 [32768, 128], P('animal')
Inputs may be any that keep to these rules, and one draw needn't show every extreme that they name: send_rows[o, d, :] lists 64 distinct local rows of owner o's 1024 animals, those sent to device d. sire_slot[i] = o * 64 + k with k < 16. dam_slot[i] = o * 64 + k with k >= 16.
All inputs are finite; a program needn't handle non-finite values.
Results may differ from a plain program's by a relative error of at most 0.0067.
Values may be sent and summed in bfloat16 or wider, within the bound.
A program may use at most 64 MiB of HBM per device.

v0:
```python
import jax
import jax.numpy as jnp
from jax import lax
from jax.sharding import PartitionSpec as P

SNPS = 32768
ITERS = 2


def cut_along(value, dim, size):
    before, after = (value.shape[:dim], value.shape[dim + 1 :])
    return jnp.moveaxis(value.reshape(*before, size, -1, *after), dim, 0)


def sum_at_owner(value, axis, dim):
    size = lax.axis_size(axis)
    blocks = lax.all_to_all(cut_along(value, dim, size), axis, 0, 0, tiled=True)
    return jnp.sum(blocks, axis=0)


def in_order(blocks, dim):
    lengths = list(blocks.shape[1:])
    lengths[dim] *= blocks.shape[0]
    return jnp.moveaxis(blocks, 0, dim).reshape(lengths)


def from_everyone(value, axis):
    size = lax.axis_size(axis)
    return lax.all_to_all(
        jnp.broadcast_to(value[None], (size, *value.shape)), axis, 0, 0, tiled=True
    )


def collect(value, axis, dim):
    return in_order(from_everyone(value, axis), dim)


def over_copies(value, axis):
    return from_everyone(value, axis).sum(axis=0)


def packed_total(arrays, axis):
    ends = [0]
    for a in arrays:
        ends.append(ends[-1] + a.size)
    so_far = over_copies(jnp.concatenate([a.ravel() for a in arrays]), axis)
    return tuple((so_far[b:e].reshape(a.shape) for a, b, e in zip(arrays, ends, ends[1:])))


def local(
    genotype,
    allele_freq,
    right_side,
    diagonal,
    mendelian,
    genomic_weight,
    send_rows,
    sire_slot,
    dam_slot,
):
    columns = right_side.shape[1]
    owners = lax.axis_size("animal")
    slots = send_rows.shape[2]
    centered = (genotype.astype(jnp.float32) - 2.0 * allele_freq[None, :]).astype(jnp.bfloat16)
    outgoing_rows = send_rows[0]
    flat_rows = outgoing_rows.reshape(-1)
    scale = genomic_weight[None, :] / SNPS

    def pedigree(field):
        width = field.shape[1]
        outgoing = field[outgoing_rows]
        incoming = lax.all_to_all(outgoing, "animal", split_axis=0, concat_axis=0, tiled=True)
        received = incoming.reshape(owners * slots, width)
        mendel_term = mendelian[:, None] * (
            field - 0.5 * (received[sire_slot] + received[dam_slot])
        )
        back = jnp.zeros((owners * slots, width), jnp.float32)
        back = back.at[sire_slot].add(-0.5 * mendel_term).at[dam_slot].add(-0.5 * mendel_term)
        returned = lax.all_to_all(
            back.reshape(owners, slots, width), "animal", split_axis=0, concat_axis=0, tiled=True
        )
        return mendel_term + jnp.zeros_like(field).at[flat_rows].add(returned.reshape(-1, width))

    def genomic(field):
        field_b = field.astype(jnp.bfloat16)
        block = centered
        owned = sum_at_owner(
            lax.dot_general(
                block, field_b, (((0,), (0,)), ((), ())), preferred_element_type=jnp.float32
            ),
            "animal",
            0,
        )
        owned_b = owned.astype(jnp.bfloat16)
        block = centered
        partial_value = jnp.dot(
            block, collect(owned_b, "animal", 0), preferred_element_type=jnp.float32
        )
        return over_copies(partial_value, "snp")

    def operate(field):
        share = columns // lax.axis_size("snp")
        begin = lax.axis_index("snp") * share
        field_share = lax.dynamic_slice_in_dim(field, begin, share, 1)
        ped = collect(pedigree(field_share), "snp", 1)
        return diagonal * field + ped + scale * genomic(field)

    solution = jnp.zeros_like(right_side)
    residual = right_side
    w_field = operate(residual)
    z_field = jnp.zeros_like(right_side)
    s_field = jnp.zeros_like(right_side)
    p_field = jnp.zeros_like(right_side)
    gamma_prev = None
    alpha_prev = None
    for step in range(ITERS):
        gamma, delta = packed_total(
            (jnp.sum(residual * residual, axis=0), jnp.sum(w_field * residual, axis=0)), "animal"
        )
        q_field = operate(w_field)
        if step == 0:
            beta = jnp.zeros_like(gamma)
            alpha = gamma / delta
        else:
            beta = gamma / gamma_prev
            alpha = gamma / (delta - beta * gamma / alpha_prev)
        z_field = q_field + beta * z_field
        s_field = w_field + beta * s_field
        p_field = residual + beta * p_field
        solution = solution + alpha * p_field
        residual = residual - alpha * s_field
        w_field = w_field - alpha * z_field
        gamma_prev = gamma
        alpha_prev = alpha
    return (solution, residual)


def solution(mesh):
    placed = (
        P("animal", "snp"),
        P("snp"),
        P("animal", None),
        P("animal", None),
        P("animal"),
        P(),
        P("animal", None, None),
        P("animal"),
        P("animal"),
    )
    return jax.shard_map(
        local,
        mesh=mesh,
        in_specs=placed,
        out_specs=(P("animal", None), P("animal", None)),
        check_vma=False,
    )
```

profile of v0, /device:TPU:1, one launch (start us, length us, event | category | flops | bytes accessed | tf_op | source)
XLA Modules:
  0.0 434.7 jit_solution(7163668507741825915)
XLA Ops:
  2.8 5.5 %gather_fusion = f32[2048,16]{1,0:T(8,128)S(1)} fusion(f32[1024,16]{1,0:T(8,128)S(1)} %constant_dynamic-slice_fusion.1, s32[2048]{0:T(1024)S(1)} %broadcast_clamp_fusion), kind=kCustom, calls=%fused_computation | custom fusion | bytes 270336 | tf_op jit(solution)/shard_map/gather | solution.py:71
  9.4 12.0 %all-to-all-start = ((f32[32,1,1024]{2,1,0:T(1,128)}), f32[32,1,1024]{2,1,0:T(1,128)S(1)}, u32[]{:S(2)}, u32[]{:S(2)}) async-start(f32[32,1,1024]{2,1,0:T(1,128)} %reshape.252), calls=%async_computation | async-start | bytes 262144 | tf_op jit(solution)/shard_map/all_to_all | solution.py:72
  21.5 7.3 %fusion.3 = f32[4096,128]{1,0:T(8,128)} fusion(bf16[1024,4096]{1,0:T(8,128)(2,1)} %param.9, f32[4096]{0:T(1024)S(1)} %broadcast_multiply_fusion, f32[1024,128]{1,0:T(8,128)S(1)} %copy-done), kind=kOutput, calls=%fused_computation.16 | convolution fusion | flops 1086455808 | bytes 11026432 | tf_op jit(solution)/shard_map/dot_general | solution.py:88
  30.8 7.5 %all-to-all-start.3 = ((f32[32,128,128]{2,1,0:T(8,128)}), f32[32,128,128]{2,1,0:T(8,128)}, u32[]{:S(2)}, u32[]{:S(2)}) async-start(f32[32,128,128]{2,1,0:T(8,128)} %bitcast.8), calls=%async_computation.3 | async-start | bytes 4194304 | tf_op jit(solution)/shard_map/all_to_all | solution.py:17
  46.1 6.3 %scatter_custom_fusion = f32[2048,16]{1,0:T(8,128)S(1)} fusion(s32[1024]{0:T(1024)S(1)} %get-tuple-element.14, f32[]{:T(128)} %constant.11.clone.1, f32[1024,16]{1,0:T(8,128)S(1)} %subtract_multiply_fusion.1, f32[]{:T(128)} %constant.3.clone.1), kind=kCustom, calls=%fused_computation.28 | custom fusion | flops 32768 | bytes 655368 | tf_op jit(solution)/shard_map/scatter-add | solution.py:78
  52.5 6.5 %scatter_custom_fusion.1 = f32[2048,16]{1,0:T(8,128)S(1)} fusion(f32[2048,16]{1,0:T(8,128)S(1)} %scatter_custom_fusion, s32[1024]{0:T(1024)S(1)} %get-tuple-element.12, f32[1024,16]{1,0:T(8,128)S(1)} %subtract_multiply_fusion.1, f32[]{:T(128)} %constant.3.clone.1), kind=kCustom, calls=%fused_computation.35 | custom fusion | flops 32768 | bytes 655364 | tf_op jit(solution)/shard_map/scatter-add | solution.py:78
  60.1 26.1 %all-to-all-done.3 = f32[32,128,128]{2,1,0:T(8,128)} async-done(((f32[32,128,128]{2,1,0:T(8,128)}), f32[32,128,128]{2,1,0:T(8,128)}, u32[]{:S(2)}, u32[]{:S(2)}) %all-to-all-start.3) | async-done | bytes 2097184 | tf_op jit(solution)/shard_map/all_to_all | solution.py:17
  86.2 6.7 %all-to-all-start.1 = ((f32[32,1,1024]{2,1,0:T(1,128)}), f32[32,1,1024]{2,1,0:T(1,128)S(1)}, u32[]{:S(2)}, u32[]{:S(2)}) async-start(f32[32,1,1024]{2,1,0:T(1,128)} %reshape.254), calls=%async_computation.1 | async-start | bytes 262144 | tf_op jit(solution)/shard_map/all_to_all | solution.py:79
  94.6 7.6 %all-to-all-done.1 = f32[32,1,1024]{2,1,0:T(1,128)S(1)} async-done(((f32[32,1,1024]{2,1,0:T(1,128)}), f32[32,1,1024]{2,1,0:T(1,128)S(1)}, u32[]{:S(2)}, u32[]{:S(2)}) %all-to-all-start.1) | async-done | bytes 131104 | tf_op jit(solution)/shard_map/all_to_all | solution.py:79
  108.8 11.9 %scatter_fusion = f32[1024,16]{1,0:T(8,128)S(1)} fusion(f32[1024,16]{1,0:T(8,128)S(1)} %subtract_multiply_fusion.1, s32[2048]{0:T(1024)S(1)} %bitcast.54, f32[2048,16]{1,0:T(8,128)S(1)} %bitcast.38), kind=kCustom, calls=%fused_computation.8 | custom fusion | flops 32768 | bytes 401408 | tf_op jit(solution)/shard_map/scatter-add | solution.py:82
  120.9 10.4 %all-to-all-done.4 = bf16[32,128,128]{2,1,0:T(8,128)(2,1)S(1)} async-done(((bf16[32,128,128]{2,1,0:T(8,128)(2,1)}), bf16[32,128,128]{2,1,0:T(8,128)(2,1)S(1)}, u32[]{:S(2)}, u32[]{:S(2)}) %all-to-all-start.4) | async-done | bytes 1048608 | tf_op jit(solution)/shard_map/all_to_all | solution.py:29
  132.1 10.4 %all-to-all-start.2 = ((f32[8,1024,16]{1,2,0:T(8,128)}), f32[8,1024,16]{1,2,0:T(8,128)S(1)}, u32[]{:S(2)}, u32[]{:S(2)}) async-start(f32[8,1024,16]{1,2,0:T(8,128)} %broadcast_in_dim.22), calls=%async_computation.2 | async-start | bytes 1048576 | tf_op jit(solution)/shard_map/all_to_all | solution.py:29
  142.5 5.7 %fusion.2 = f32[1024,128]{1,0:T(8,128)S(1)} fusion(bf16[4096,128]{1,0:T(8,128)(2,1)S(1)} %bitcast.53, bf16[1024,4096]{1,0:T(8,128)(2,1)} %param.9, f32[4096]{0:T(1024)S(1)} %broadcast_multiply_fusion), kind=kOutput, calls=%fused_computation.15 | convolution fusion | flops 1086324736 | bytes 9977856 | tf_op jit(solution)/shard_map/dot_general | solution.py:96
  154.2 5.3 %all-to-all-start.5 = ((f32[8,1024,128]{2,1,0:T(8,128)}), f32[8,1024,128]{2,1,0:T(8,128)}, u32[]{:S(2)}, u32[]{:S(2)}) async-start(f32[8,1024,128]{2,1,0:T(8,128)} %broadcast_in_dim.24), calls=%async_computation.5 | async-start | bytes 8388608 | tf_op jit(solution)/shard_map/all_to_all | solution.py:29
  159.7 48.7 %all-to-all-done.5 = f32[8,1024,128]{2,1,0:T(8,128)} async-done(((f32[8,1024,128]{2,1,0:T(8,128)}), f32[8,1024,128]{2,1,0:T(8,128)}, u32[]{:S(2)}, u32[]{:S(2)}) %all-to-all-start.5) | async-done | bytes 4194336 | tf_op jit(solution)/shard_map/all_to_all | solution.py:29
  216.2 5.5 %gather_fusion.3 = f32[2048,16]{1,0:T(8,128)S(1)} fusion(f32[1024,16]{1,0:T(8,128)S(1)} %constant_dynamic-slice_fusion, s32[2048]{0:T(1024)S(1)} %broadcast_clamp_fusion), kind=kCustom, calls=%fused_computation.3 | custom fusion | bytes 270336 | tf_op jit(solution)/shard_map/gather | solution.py:71
  224.7 7.4 %all-to-all-start.7 = ((f32[32,1,1024]{2,1,0:T(1,128)}), f32[32,1,1024]{2,1,0:T(1,128)S(1)}, u32[]{:S(2)}, u32[]{:S(2)}) async-start(f32[32,1,1024]{2,1,0:T(1,128)} %reshape.256), calls=%async_computation.7 | async-start | bytes 262144 | tf_op jit(solution)/shard_map/all_to_all | solution.py:72
  232.1 7.3 %fusion.1 = f32[4096,128]{1,0:T(8,128)} fusion(bf16[1024,4096]{1,0:T(8,128)(2,1)} %param.9, f32[4096]{0:T(1024)S(1)} %broadcast_multiply_fusion, f32[1024,128]{1,0:T(8,128)S(1)} %get-tuple-element.9), kind=kOutput, calls=%fused_computation.14 | convolution fusion | flops 1086455808 | bytes 11026432 | tf_op jit(solution)/shard_map/dot_general | solution.py:88
  241.4 7.5 %all-to-all-start.10 = ((f32[32,128,128]{2,1,0:T(8,128)}), f32[32,128,128]{2,1,0:T(8,128)}, u32[]{:S(2)}, u32[]{:S(2)}) async-start(f32[32,128,128]{2,1,0:T(8,128)} %bitcast.16), calls=%async_computation.10 | async-start | bytes 4194304 | tf_op jit(solution)/shard_map/all_to_all | solution.py:17
  258.5 6.3 %scatter_custom_fusion.3 = f32[2048,16]{1,0:T(8,128)S(1)} fusion(s32[1024]{0:T(1024)S(1)} %get-tuple-element.14, f32[]{:T(128)} %constant.11.clone.1, f32[1024,16]{1,0:T(8,128)S(1)} %subtract_multiply_fusion, f32[]{:T(128)} %constant.3.clone.1), kind=kCustom, calls=%fused_computation.26 | custom fusion | flops 32768 | bytes 655368 | tf_op jit(solution)/shard_map/scatter-add | solution.py:78
  264.8 6.5 %scatter_custom_fusion.4 = f32[2048,16]{1,0:T(8,128)S(1)} fusion(f32[2048,16]{1,0:T(8,128)S(1)} %scatter_custom_fusion.3, s32[1024]{0:T(1024)S(1)} %get-tuple-element.12, f32[1024,16]{1,0:T(8,128)S(1)} %subtract_multiply_fusion, f32[]{:T(128)} %constant.3.clone.1), kind=kCustom, calls=%fused_computation.32 | custom fusion | flops 32768 | bytes 655364 | tf_op jit(solution)/shard_map/scatter-add | solution.py:78
  272.5 22.2 %all-to-all-done.10 = f32[32,128,128]{2,1,0:T(8,128)} async-done(((f32[32,128,128]{2,1,0:T(8,128)}), f32[32,128,128]{2,1,0:T(8,128)}, u32[]{:S(2)}, u32[]{:S(2)}) %all-to-all-start.10) | async-done | bytes 2097184 | tf_op jit(solution)/shard_map/all_to_all | solution.py:17
  294.7 7.8 %all-to-all-start.8 = ((f32[32,1,1024]{2,1,0:T(1,128)}), f32[32,1,1024]{2,1,0:T(1,128)S(1)}, u32[]{:S(2)}, u32[]{:S(2)}) async-start(f32[32,1,1024]{2,1,0:T(1,128)} %reshape.258), calls=%async_computation.8 | async-start | bytes 262144 | tf_op jit(solution)/shard_map/all_to_all | solution.py:79
  304.2 7.6 %all-to-all-done.8 = f32[32,1,1024]{2,1,0:T(1,128)S(1)} async-done(((f32[32,1,1024]{2,1,0:T(1,128)}), f32[32,1,1024]{2,1,0:T(1,128)S(1)}, u32[]{:S(2)}, u32[]{:S(2)}) %all-to-all-start.8) | async-done | bytes 131104 | tf_op jit(solution)/shard_map/all_to_all | solution.py:79
  313.1 4.7 %all-to-all-start.11 = ((bf16[32,128,128]{2,1,0:T(8,128)(2,1)}), bf16[32,128,128]{2,1,0:T(8,128)(2,1)}, u32[]{:S(2)}, u32[]{:S(2)}) async-start(bf16[32,128,128]{2,1,0:T(8,128)(2,1)} %broadcast_in_dim.27), calls=%async_computation.11 | async-start | bytes 2097152 | tf_op jit(solution)/shard_map/all_to_all | solution.py:29
  319.1 11.7 %scatter_fusion.1 = f32[1024,16]{1,0:T(8,128)S(1)} fusion(f32[1024,16]{1,0:T(8,128)S(1)} %subtract_multiply_fusion, s32[2048]{0:T(1024)S(1)} %bitcast.55, f32[2048,16]{1,0:T(8,128)S(1)} %bitcast.37), kind=kCustom, calls=%fused_computation.11 | custom fusion | flops 32768 | bytes 401408 | tf_op jit(solution)/shard_map/scatter-add | solution.py:82
  331.0 9.7 %all-to-all-done.11 = bf16[32,128,128]{2,1,0:T(8,128)(2,1)} async-done(((bf16[32,128,128]{2,1,0:T(8,128)(2,1)}), bf16[32,128,128]{2,1,0:T(8,128)(2,1)}, u32[]{:S(2)}, u32[]{:S(2)}) %all-to-all-start.11) | async-done | bytes 1048608 | tf_op jit(solution)/shard_map/all_to_all | solution.py:29
  341.5 9.8 %all-to-all-start.9 = ((f32[8,1024,16]{1,2,0:T(8,128)}), f32[8,1024,16]{1,2,0:T(8,128)S(1)}, u32[]{:S(2)}, u32[]{:S(2)}) async-start(f32[8,1024,16]{1,2,0:T(8,128)} %broadcast_in_dim.26), calls=%async_computation.9 | async-start | bytes 1048576 | tf_op jit(solution)/shard_map/all_to_all | solution.py:29
  351.3 6.0 %fusion = f32[1024,128]{1,0:T(8,128)S(1)} fusion(bf16[4096,128]{1,0:T(8,128)(2,1)} %bitcast.17, bf16[1024,4096]{1,0:T(8,128)(2,1)} %param.9, f32[4096]{0:T(1024)S(1)} %broadcast_multiply_fusion), kind=kOutput, calls=%fused_computation.13 | convolution fusion | flops 1086324736 | bytes 9977856 | tf_op jit(solution)/shard_map/dot_general | solution.py:96
  363.0 5.3 %all-to-all-start.12 = ((f32[8,1024,128]{2,1,0:T(8,128)}), f32[8,1024,128]{2,1,0:T(8,128)}, u32[]{:S(2)}, u32[]{:S(2)}) async-start(f32[8,1024,128]{2,1,0:T(8,128)} %broadcast_in_dim.28), calls=%async_computation.12 | async-start | bytes 8388608 | tf_op jit(solution)/shard_map/all_to_all | solution.py:29
  368.6 48.7 %all-to-all-done.12 = f32[8,1024,128]{2,1,0:T(8,128)} async-done(((f32[8,1024,128]{2,1,0:T(8,128)}), f32[8,1024,128]{2,1,0:T(8,128)}, u32[]{:S(2)}, u32[]{:S(2)}) %all-to-all-start.12) | async-done | bytes 4194336 | tf_op jit(solution)/shard_map/all_to_all | solution.py:29
  420.0 13.5 %all_to_all.72 = f32[32,1,256]{2,1,0:T(1,128)S(1)} all-to-all(f32[32,1,256]{2,1,0:T(1,128)S(1)} %broadcast_in_dim.29), channel_id=1, replica_groups=mesh['animal'=32,'snp'=8] {'animal'}, dimensions={0} | all-to-all | bytes 65536 | tf_op jit(solution)/shard_map/all_to_all | solution.py:29
  (86 shorter events, 68.5 us)
Async XLA Ops:
  0.6 20.8 %copy-start = (f32[1024,128]{1,0:T(8,128)S(1)}, f32[1024,128]{1,0:T(8,128)}, u32[]{:S(2)}) copy-start(f32[1024,128]{1,0:T(8,128)} %param.11) | copy-start | bytes 1572868
  0.6 20.8 %copy-start.4 = (f32[4096]{0:T(1024)S(1)}, f32[4096]{0:T(1024)}, u32[]{:S(2)}) copy-start(f32[4096]{0:T(1024)} %param.10) | copy-start | bytes 49156
  9.4 21.4 %all-to-all-start = ((f32[32,1,1024]{2,1,0:T(1,128)}), f32[32,1,1024]{2,1,0:T(1,128)S(1)}, u32[]{:S(2)}, u32[]{:S(2)}) async-start(f32[32,1,1024]{2,1,0:T(1,128)} %reshape.252), calls=%async_computation | async-start | bytes 262144 | tf_op jit(solution)/shard_map/all_to_all | solution.py:72
  21.5 16.8 %copy-start.5 = (s32[1024]{0:T(1024)S(1)}, s32[1024]{0:T(1024)}, u32[]{:S(2)}) copy-start(s32[1024]{0:T(1024)} %param.16) | copy-start | bytes 12292
  21.5 16.8 %copy-start.6 = (s32[1024]{0:T(1024)S(1)}, s32[1024]{0:T(1024)}, u32[]{:S(2)}) copy-start(s32[1024]{0:T(1024)} %param.17) | copy-start | bytes 12292
  28.8 17.0 %copy-start.3 = (f32[1024]{0:T(1024)S(1)}, f32[1024]{0:T(1024)}, u32[]{:S(2)}) copy-start(f32[1024]{0:T(1024)} %param.13) | copy-start | bytes 12292
  30.8 55.4 %all-to-all-start.3 = ((f32[32,128,128]{2,1,0:T(8,128)}), f32[32,128,128]{2,1,0:T(8,128)}, u32[]{:S(2)}, u32[]{:S(2)}) async-start(f32[32,128,128]{2,1,0:T(8,128)} %bitcast.8), calls=%async_computation.3 | async-start | bytes 4194304 | tf_op jit(solution)/shard_map/all_to_all | solution.py:17
  43.0 64.4 %copy-start.2 = (s32[1,32,64]{2,1,0:T(8,128)S(1)}, s32[1,32,64]{2,1,0:T(8,128)}, u32[]{:S(2)}) copy-start(s32[1,32,64]{2,1,0:T(8,128)} %param.15) | copy-start | bytes 24580
  86.2 16.0 %all-to-all-start.1 = ((f32[32,1,1024]{2,1,0:T(1,128)}), f32[32,1,1024]{2,1,0:T(1,128)S(1)}, u32[]{:S(2)}, u32[]{:S(2)}) async-start(f32[32,1,1024]{2,1,0:T(1,128)} %reshape.254), calls=%async_computation.1 | async-start | bytes 262144 | tf_op jit(solution)/shard_map/all_to_all | solution.py:79
  103.4 27.8 %all-to-all-start.4 = ((bf16[32,128,128]{2,1,0:T(8,128)(2,1)}), bf16[32,128,128]{2,1,0:T(8,128)(2,1)S(1)}, u32[]{:S(2)}, u32[]{:S(2)}) async-start(bf16[32,128,128]{2,1,0:T(8,128)(2,1)} %broadcast_in_dim.23), calls=%async_computation.4 | async-start | bytes 2097152 | tf_op jit(solution)/shard_map/all_to_all | solution.py:29
  132.1 19.9 %all-to-all-start.2 = ((f32[8,1024,16]{1,2,0:T(8,128)}), f32[8,1024,16]{1,2,0:T(8,128)S(1)}, u32[]{:S(2)}, u32[]{:S(2)}) async-start(f32[8,1024,16]{1,2,0:T(8,128)} %broadcast_in_dim.22), calls=%async_computation.2 | async-start | bytes 1048576 | tf_op jit(solution)/shard_map/all_to_all | solution.py:29
  148.2 11.3 %copy-start.7 = (f32[128]{0:T(128)S(1)}, f32[128]{0:T(128)}, u32[]{:S(2)}) copy-start(f32[128]{0:T(128)} %param.14) | copy-start | bytes 1540
  148.2 62.7 %copy-start.1 = (f32[1024,128]{1,0:T(8,128)S(1)}, f32[1024,128]{1,0:T(8,128)}, u32[]{:S(2)}) copy-start(f32[1024,128]{1,0:T(8,128)} %param.12) | copy-start | bytes 1572868
  154.2 54.2 %all-to-all-start.5 = ((f32[8,1024,128]{2,1,0:T(8,128)}), f32[8,1024,128]{2,1,0:T(8,128)}, u32[]{:S(2)}, u32[]{:S(2)}) async-start(f32[8,1024,128]{2,1,0:T(8,128)} %broadcast_in_dim.24), calls=%async_computation.5 | async-start | bytes 8388608 | tf_op jit(solution)/shard_map/all_to_all | solution.py:29
  211.7 13.0 %all-to-all-start.6 = ((f32[32,1,256]{2,1,0:T(1,128)}), f32[32,1,256]{2,1,0:T(1,128)S(1)}, u32[]{:S(2)}, u32[]{:S(2)}) async-start(f32[32,1,256]{2,1,0:T(1,128)} %broadcast_in_dim.25), calls=%async_computation.6 | async-start | bytes 65536 | tf_op jit(solution)/shard_map/all_to_all | solution.py:29
  224.7 16.7 %all-to-all-start.7 = ((f32[32,1,1024]{2,1,0:T(1,128)}), f32[32,1,1024]{2,1,0:T(1,128)S(1)}, u32[]{:S(2)}, u32[]{:S(2)}) async-start(f32[32,1,1024]{2,1,0:T(1,128)} %reshape.256), calls=%async_computation.7 | async-start | bytes 262144 | tf_op jit(solution)/shard_map/all_to_all | solution.py:72
  241.4 53.2 %all-to-all-start.10 = ((f32[32,128,128]{2,1,0:T(8,128)}), f32[32,128,128]{2,1,0:T(8,128)}, u32[]{:S(2)}, u32[]{:S(2)}) async-start(f32[32,128,128]{2,1,0:T(8,128)} %bitcast.16), calls=%async_computation.10 | async-start | bytes 4194304 | tf_op jit(solution)/shard_map/all_to_all | solution.py:17
  294.7 17.2 %all-to-all-start.8 = ((f32[32,1,1024]{2,1,0:T(1,128)}), f32[32,1,1024]{2,1,0:T(1,128)S(1)}, u32[]{:S(2)}, u32[]{:S(2)}) async-start(f32[32,1,1024]{2,1,0:T(1,128)} %reshape.258), calls=%async_computation.8 | async-start | bytes 262144 | tf_op jit(solution)/shard_map/all_to_all | solution.py:79
  313.1 27.5 %all-to-all-start.11 = ((bf16[32,128,128]{2,1,0:T(8,128)(2,1)}), bf16[32,128,128]{2,1,0:T(8,128)(2,1)}, u32[]{:S(2)}, u32[]{:S(2)}) async-start(bf16[32,128,128]{2,1,0:T(8,128)(2,1)} %broadcast_in_dim.27), calls=%async_computation.11 | async-start | bytes 2097152 | tf_op jit(solution)/shard_map/all_to_all | solution.py:29
  341.5 19.3 %all-to-all-start.9 = ((f32[8,1024,16]{1,2,0:T(8,128)}), f32[8,1024,16]{1,2,0:T(8,128)S(1)}, u32[]{:S(2)}, u32[]{:S(2)}) async-start(f32[8,1024,16]{1,2,0:T(8,128)} %broadcast_in_dim.26), calls=%async_computation.9 | async-start | bytes 1048576 | tf_op jit(solution)/shard_map/all_to_all | solution.py:29
  363.0 54.2 %all-to-all-start.12 = ((f32[8,1024,128]{2,1,0:T(8,128)}), f32[8,1024,128]{2,1,0:T(8,128)}, u32[]{:S(2)}, u32[]{:S(2)}) async-start(f32[8,1024,128]{2,1,0:T(8,128)} %broadcast_in_dim.28), calls=%async_computation.12 | async-start | bytes 8388608 | tf_op jit(solution)/shard_map/all_to_all | solution.py:29
where the time goes:
time: 436 us; the launch traced here: 435 us
  waiting for transfers between devices  194 us (44%)
  starting transfers between devices  92.5 us (21%)
  other arithmetic  65.1 us (15%)
  local copies, waits for them, and re-layouts  42 us (10%)
  matrix products  26.2 us (6%)
  blocking collectives  13.5 us (3%)
    all_to_all x7, waiting for transfers between devices, from_everyone(): lax.all_to_all(jnp.broadcast_to(value[None], (size, *value.shape)), axis,...  127 us
    all_to_all x2, waiting for transfers between devices, sum_at_owner(): blocks = lax.all_to_all(cut_along(value, dim, size), axis, 0, 0, tiled=True)  48.3 us
    all_to_all x7, starting transfers between devices, from_everyone(): lax.all_to_all(jnp.broadcast_to(value[None], (size, *value.shape)), axis,...  43.7 us
    scatter-add x4, other arithmetic, pedigree(): back.at[sire_slot].add(-0.5 * mendel_term).at[dam_slot]  25.6 us
    scatter-add x2, other arithmetic, pedigree(): jnp.zeros_like(field).at[flat_rows].add(returned.reshape(-1, width))  23.6 us
    all_to_all x2, starting transfers between devices, pedigree(): lax.all_to_all(outgoing, 'animal', split_axis=0, concat_axis=0, tiled=True)  19.4 us
    all_to_all x2, waiting for transfers between devices, pedigree(): lax.all_to_all(back.reshape(owners, slots, width), 'animal', split_axis=0...  15.3 us
    all_to_all x2, starting transfers between devices, sum_at_owner(): blocks = lax.all_to_all(cut_along(value, dim, size), axis, 0, 0, tiled=True)  15 us
  transfers between devices with their start and end apart: 13, of which 13 were waited for; matrix products, arithmetic and copies ran while one was open for 25% of the time, Pallas kernels for 0%

commit v1 on v0

v1 whole, which is shorter than its diff:
```python
import functools

import jax
import jax.numpy as jnp
from jax import lax
from jax.experimental import pallas as pl
from jax.experimental.pallas import tpu as pltpu
from jax.sharding import PartitionSpec as P

MESH = pl.DeviceIdType.MESH
SNPS = 32768
Z, Y, S = 8, 4, 8
OWN = Z * Y
COLS, ROWS, LOCAL = 128, 1024, 4096
SHARE = COLS // S
ZSHARE = COLS // Z
YCH = LOCAL // Y
SUBS = 2
SUB = YCH // SUBS
SLOTS = 64
NT = (((1,), (1,)), ((), ()))
F32, BF16 = jnp.float32, jnp.bfloat16


def dot(a, b):
    return jnp.dot(a, b, preferred_element_type=F32)


def dot_nt(a, b):
    return lax.dot_general(a, b, NT, preferred_element_type=F32)


def halves(value):
    high = value.astype(BF16)
    low = (value - high.astype(F32)).astype(BF16)
    return jnp.concatenate([high, low], axis=0)


def swap(value):
    return pltpu.roll(value, SLOTS, 1)


def kernel(
    geno, freq, rhs, diag, mend, weight, rows, sire, dam,
    x_out, r_out,
    block, send_hot, parent_hot, field, field_t, diag_t,
    y_own, y_send, y_recv, z_own, z_send, z_recv, effects,
    g_own, g_send, g_recv, p_send, p_recv, p_mat, dot_send, dot_recv, final,
    load_sem, y_s, y_r, z_s, z_r, zg_s, zg_r, yg_s, yg_r, g_s, g_r, x_s, x_r,
    p_s, p_r, d_s, d_r, f_s, f_r,
):
    a, s = lax.axis_index("animal"), lax.axis_index("snp")
    z, y = a // Y, a % Y

    def at_y(k):
        return (z * Y + (y + k) % Y, s)

    def at_z(k):
        return (((z + k) % Z) * Y + y, s)

    def at_s(k):
        return (a, (s + k) % S)

    def at_a(k):
        return ((a + k) % OWN, s)

    def remote(src, dst, send_sem, recv_sem, peer):
        return pltpu.make_async_remote_copy(
            src_ref=src, dst_ref=dst, send_sem=send_sem, recv_sem=recv_sem,
            device_id=peer, device_id_type=MESH,
        )

    def settle(ref, send_sem, recv_sem, peer):
        return remote(ref, ref, send_sem, recv_sem, peer)

    def y_lanes(which, sub):
        return pl.ds(pl.multiple_of(which * YCH + sub * SUB, SUB), SUB)

    def loads(which):
        lanes = pl.ds(pl.multiple_of(which * YCH, YCH), YCH)
        return pltpu.make_async_copy(geno.at[:, lanes], block.at[:, lanes], load_sem.at[which])

    for k in range(1, Y + 1):
        loads((y + k) % Y).start()

    barrier = pltpu.get_barrier_semaphore()

    def greet_a(k, carry):
        pl.semaphore_signal(barrier, inc=1, device_id=at_a(k), device_id_type=MESH)
        return carry

    def greet_s(k, carry):
        pl.semaphore_signal(barrier, inc=1, device_id=at_s(k), device_id_type=MESH)
        return carry

    lax.fori_loop(1, OWN, greet_a, 0)
    lax.fori_loop(1, S, greet_s, 0)

    field_t[...] = rhs[...].T
    diag_t[...] = diag[...].T
    field[0] = field_t[...].astype(BF16)
    mine = pl.ds(pl.multiple_of(s * SHARE, SHARE), SHARE)
    z_mine = pl.ds(pl.multiple_of(z * ZSHARE, ZSHARE), ZSHARE)
    b_share = field_t[mine, :]
    d_share = diag_t[mine, :]
    scale = weight[mine, :] * (1.0 / SNPS)
    lane = lax.broadcasted_iota(jnp.int32, (SHARE, 2 * SLOTS), 1)
    first = lane < SLOTS

    pl.semaphore_wait(barrier, OWN - 1 + S - 1)

    def centre(which):
        loads(which).wait()

        def rows_of(i, carry):
            at = pl.ds(pl.multiple_of(i * 64, 64), 64)
            lanes = pl.ds(pl.multiple_of(which * YCH, YCH), YCH)
            block[at, lanes] = (block[at, lanes].astype(F32) - 2.0 * freq[:, lanes]).astype(BF16)
            return carry

        lax.fori_loop(0, ROWS // 64, rows_of, 0)

    def effects_out(op):
        def one(k, carry):
            which = (y + k) % Y
            if op == 0:
                centre(which)

            def part(sub, inner):
                here = pl.ds(pl.multiple_of(sub * SUB, SUB), SUB)
                value = dot(field[op], block[:, y_lanes(which, sub)])
                y_send[op, which, :, here] = value.astype(BF16)
                remote(
                    y_send.at[op, which, :, here], y_recv.at[op, y, :, here],
                    y_s.at[op, k - 1, sub], y_r.at[op, y, sub], at_y(k),
                ).start()
                return inner

            lax.fori_loop(0, SUBS, part, 0)
            return carry

        lax.fori_loop(1, Y, one, 0)
        if op == 0:
            centre(y)
        for sub in range(SUBS):
            y_own[:, sub * SUB : (sub + 1) * SUB] = dot(field[op], block[:, y_lanes(y, sub)])

    def effects_mid(op):
        for sub in range(SUBS):
            here = slice(sub * SUB, (sub + 1) * SUB)
            total = y_own[:, here]
            for k in range(1, Y):
                which = (y + k) % Y
                piece = y_recv.at[op, which, :, here]
                settle(piece, y_s.at[op, k - 1, sub], y_r.at[op, which, sub], at_y(k)).wait_recv()
                total = total + piece[...].astype(F32)
            z_own[:, here] = total
            z_send[op, :, here] = total.astype(BF16)

            def give(k, carry):
                peer_rows = pl.ds(pl.multiple_of(((z + k) % Z) * ZSHARE, ZSHARE), ZSHARE)
                remote(
                    z_send.at[op, peer_rows, here], z_recv.at[op, z, :, here],
                    z_s.at[op, sub], z_r.at[op, sub], at_z(k),
                ).start()
                return carry

            lax.fori_loop(1, Z, give, 0)

    def effects_sum(op):
        for sub in range(SUBS):
            here = slice(sub * SUB, (sub + 1) * SUB)
            settle(
                z_recv.at[op, 0 : Z - 1, :, here], z_s.at[op, sub], z_r.at[op, sub], at_z(1)
            ).wait_recv()
            total = z_own[z_mine, here]
            for k in range(1, Z):
                total = total + z_recv[op, (z + k) % Z, :, here].astype(F32)
            effects[op, z_mine, y_lanes(y, sub)] = total.astype(BF16)

            def give(k, carry):
                piece = effects.at[op, z_mine, y_lanes(y, sub)]
                remote(piece, piece, zg_s.at[op, sub], zg_r.at[op, sub], at_z(k)).start()
                return carry

            lax.fori_loop(1, Z, give, 0)

    def effects_spread(op):
        for sub in range(SUBS):
            settle(
                effects.at[op, 0 : COLS - ZSHARE, y_lanes(y, sub)],
                zg_s.at[op, sub], zg_r.at[op, sub], at_z(1),
            ).wait_recv()
            for k in range(1, Y):
                piece = effects.at[op, :, y_lanes(y, sub)]
                remote(
                    piece, piece, yg_s.at[op, k - 1, sub], yg_r.at[op, y, sub], at_y(k)
                ).start()

    def genomic_own(op):
        lanes = pl.ds(pl.multiple_of(y * YCH, YCH), YCH)
        g_own[...] = dot_nt(effects[op, :, lanes], block[:, lanes])

    def genomic(op):
        for sub in range(SUBS):
            for k in range(1, Y):
                which = (y + k) % Y
                lanes = y_lanes(which, sub)
                piece = effects.at[op, :, lanes]
                settle(piece, yg_s.at[op, k - 1, sub], yg_r.at[op, which, sub], at_y(k)).wait_recv()
                g_own[...] += dot_nt(piece[...], block[:, lanes])
        g_send[op] = g_own[...].astype(BF16)

        def give(k, carry):
            peer_rows = pl.ds(pl.multiple_of(((s + k) % S) * SHARE, SHARE), SHARE)
            remote(
                g_send.at[op, peer_rows, :], g_recv.at[op, s], g_s.at[op], g_r.at[op], at_s(k)
            ).start()
            return carry

        lax.fori_loop(1, S, give, 0)
        settle(g_recv.at[op, 0 : S - 1], g_s.at[op], g_r.at[op], at_s(1)).wait_recv()
        total = g_own[mine, :]
        for k in range(1, S):
            total = total + g_recv[op, (s + k) % S].astype(F32)
        return total

    def relay_out(leg, op, value):
        both = value
        for pair in range(OWN // 2):
            lanes = slice(pair * 2 * SLOTS, (pair + 1) * 2 * SLOTS)
            high, low = both[:SHARE, lanes], both[SHARE:, lanes]
            p_send[op, leg, 2 * pair] = jnp.where(first, high, swap(low)).astype(BF16)
            p_send[op, leg, 2 * pair + 1] = jnp.where(first, swap(high), low).astype(BF16)

        def give(k, carry):
            peer = (a + k) % OWN
            remote(
                p_send.at[op, leg, peer], p_recv.at[op, leg, a],
                p_s.at[op, leg], p_r.at[op, leg], at_a(k),
            ).start()
            return carry

        lax.fori_loop(1, OWN, give, 0)

    def relay_in(leg, op):
        settle(
            p_recv.at[op, leg, 0 : OWN - 1], p_s.at[op, leg], p_r.at[op, leg], at_a(1)
        ).wait_recv()
        p_recv[op, leg, a] = p_send[op, leg, a]
        for pair in range(OWN // 2):
            lanes = slice(pair * 2 * SLOTS, (pair + 1) * 2 * SLOTS)
            one = p_recv[op, leg, 2 * pair].astype(F32)
            two = p_recv[op, leg, 2 * pair + 1].astype(F32)
            p_mat[:SHARE, lanes] = jnp.where(first, one, swap(two)).astype(BF16)
            p_mat[SHARE:, lanes] = jnp.where(first, swap(one), two).astype(BF16)
        return p_mat[...]

    def fold(both):
        return both[:SHARE] + both[SHARE:]

    def make_send_hot():
        even = rows[pl.ds(0, OWN // 2, stride=2), :]
        odd = rows[pl.ds(1, OWN // 2, stride=2), :]
        pairs = jnp.concatenate([even, odd], axis=1)
        at = lax.broadcasted_iota(jnp.int32, (ROWS, 2 * SLOTS), 0)
        for pair in range(OWN // 2):
            lanes = slice(pair * 2 * SLOTS, (pair + 1) * 2 * SLOTS)
            send_hot[:, lanes] = (at == pairs[pair : pair + 1, :]).astype(F32).astype(BF16)

    def make_parent_hot():
        def some(i, carry):
            at = lax.broadcasted_iota(jnp.int32, (128, ROWS), 0) + i * 128
            here = (at == sire[...]) | (at == dam[...])
            parent_hot[pl.ds(pl.multiple_of(i * 128, 128), 128), :] = here.astype(F32).astype(BF16)
            return carry

        lax.fori_loop(0, OWN * SLOTS // 128, some, 0)

    def pedigree_out(op, value):
        relay_out(0, op, dot(halves(value), send_hot[...]))

    def pedigree_mid(op, value):
        parents = fold(dot(relay_in(0, op), parent_hot[...]))
        term = mend[...] * (value - 0.5 * parents)
        back = -0.5 * fold(dot_nt(halves(term), parent_hot[...]))
        high = back.astype(BF16).astype(F32)
        relay_out(1, op, jnp.concatenate([high, back - high], axis=0))
        return term

    def pedigree_end(op, term):
        return term + fold(dot_nt(relay_in(1, op), send_hot[...]))

    def share_field(value):
        field[1, mine, :] = value.astype(BF16)

        def give(k, carry):
            piece = field.at[1, mine, :]
            remote(piece, piece, x_s, x_r, at_s(k)).start()
            return carry

        lax.fori_loop(1, S, give, 0)

    def field_arrives():
        settle(field.at[1, 0 : COLS - SHARE, :], x_s, x_r, at_s(1)).wait_recv()

    def dots_out(batch, one, two):
        tile = jnp.where(
            lane == 0,
            jnp.sum(one, axis=1, keepdims=True),
            jnp.where(lane == 1, jnp.sum(two, axis=1, keepdims=True), 0.0),
        )
        dot_send[batch] = tile

        def give(k, carry):
            remote(
                dot_send.at[batch], dot_recv.at[batch, a], d_s.at[batch], d_r.at[batch], at_a(k)
            ).start()
            return carry

        lax.fori_loop(1, OWN, give, 0)

    def dots_in(batch):
        settle(dot_recv.at[batch, 0 : OWN - 1], d_s.at[batch], d_r.at[batch], at_a(1)).wait_recv()
        dot_recv[batch, a] = dot_send[batch]
        total = jnp.sum(dot_recv[batch], axis=0)
        return total[:, 0:1], total[:, 1:2]

    effects_out(0)
    make_send_hot()
    pedigree_out(0, b_share)
    make_parent_hot()
    effects_mid(0)
    term = pedigree_mid(0, b_share)
    effects_sum(0)
    effects_spread(0)
    genomic_own(0)
    ped = pedigree_end(0, term)
    w_share = d_share * b_share + ped + scale * genomic(0)
    share_field(w_share)
    dots_out(0, b_share * b_share, w_share * b_share)
    pedigree_out(1, w_share)
    field_arrives()

    effects_out(1)
    gamma0, delta0 = dots_in(0)
    alpha0 = gamma0 / delta0
    r_share = b_share - alpha0 * w_share
    dots_out(1, r_share * r_share, r_share * w_share)
    term = pedigree_mid(1, w_share)
    effects_mid(1)
    effects_sum(1)
    effects_spread(1)
    genomic_own(1)
    ped = pedigree_end(1, term)
    gamma1, _ = dots_in(1)
    q_share = d_share * w_share + ped + scale * genomic(1)
    w1_share = w_share - alpha0 * q_share
    dots_out(2, w1_share * r_share, w1_share)
    delta1, _ = dots_in(2)
    beta = gamma1 / gamma0
    alpha1 = gamma1 / (delta1 - beta * gamma1 / alpha0)
    final[0, mine, :] = alpha0 * b_share + alpha1 * (r_share + beta * b_share)
    final[1, mine, :] = r_share - alpha1 * (w1_share + beta * w_share)

    def give(k, carry):
        piece = final.at[:, mine, :]
        remote(piece, piece, f_s, f_r, at_s(k)).start()
        return carry

    lax.fori_loop(1, S, give, 0)
    settle(final.at[:, 0 : COLS - SHARE, :], f_s, f_r, at_s(1)).wait()
    x_out[...] = final[0]
    r_out[...] = final[1]

    for op in range(2):
        for sub in range(SUBS):
            here = slice(sub * SUB, (sub + 1) * SUB)
            for k in range(1, Y):
                settle(
                    y_send.at[op, 0, :, here], y_s.at[op, k - 1, sub], y_r.at[op, 0, sub], at_y(k)
                ).wait_send()
                settle(
                    effects.at[op, :, y_lanes(y, sub)],
                    yg_s.at[op, k - 1, sub], yg_r.at[op, 0, sub], at_y(k),
                ).wait_send()
            settle(
                z_send.at[op, 0 : COLS - ZSHARE, here], z_s.at[op, sub], z_r.at[op, sub], at_z(1)
            ).wait_send()
            settle(
                effects.at[op, 0 : COLS - ZSHARE, y_lanes(y, sub)],
                zg_s.at[op, sub], zg_r.at[op, sub], at_z(1),
            ).wait_send()
        settle(g_send.at[op, 0 : COLS - SHARE, :], g_s.at[op], g_r.at[op], at_s(1)).wait_send()
        for leg in range(2):
            settle(
                p_recv.at[op, leg, 0 : OWN - 1], p_s.at[op, leg], p_r.at[op, leg], at_a(1)
            ).wait_send()
    settle(field.at[1, 0 : COLS - SHARE, :], x_s, x_r, at_s(1)).wait_send()
    for batch in range(3):
        settle(
            dot_recv.at[batch, 0 : OWN - 1], d_s.at[batch], d_r.at[batch], at_a(1)
        ).wait_send()


def local(geno, freq, rhs, diag, mend, weight, send_rows, sire, dam):
    vmem = pl.BlockSpec(memory_space=pltpu.VMEM)
    dma = pltpu.SemaphoreType.DMA
    x_t, r_t = pl.pallas_call(
        kernel,
        out_shape=(jax.ShapeDtypeStruct((COLS, ROWS), F32),) * 2,
        in_specs=[pl.BlockSpec(memory_space=pl.ANY)] + [vmem] * 8,
        out_specs=(vmem, vmem),
        scratch_shapes=[
            pltpu.VMEM((ROWS, LOCAL), BF16),
            pltpu.VMEM((ROWS, OWN * SLOTS), BF16),
            pltpu.VMEM((OWN * SLOTS, ROWS), BF16),
            pltpu.VMEM((2, COLS, ROWS), BF16),
            pltpu.VMEM((COLS, ROWS), F32),
            pltpu.VMEM((COLS, ROWS), F32),
            pltpu.VMEM((COLS, YCH), F32),
            pltpu.VMEM((2, Y, COLS, YCH), BF16),
            pltpu.VMEM((2, Y, COLS, YCH), BF16),
            pltpu.VMEM((COLS, YCH), F32),
            pltpu.VMEM((2, COLS, YCH), BF16),
            pltpu.VMEM((2, Z, ZSHARE, YCH), BF16),
            pltpu.VMEM((2, COLS, LOCAL), BF16),
            pltpu.VMEM((COLS, ROWS), F32),
            pltpu.VMEM((2, COLS, ROWS), BF16),
            pltpu.VMEM((2, S, SHARE, ROWS), BF16),
            pltpu.VMEM((2, 2, OWN, SHARE, 2 * SLOTS), BF16),
            pltpu.VMEM((2, 2, OWN, SHARE, 2 * SLOTS), BF16),
            pltpu.VMEM((2 * SHARE, OWN * SLOTS), BF16),
            pltpu.VMEM((3, SHARE, 128), F32),
            pltpu.VMEM((3, OWN, SHARE, 128), F32),
            pltpu.VMEM((2, COLS, ROWS), F32),
            dma((Y,)),
            dma((2, Y - 1, SUBS)), dma((2, Y, SUBS)),
            dma((2, SUBS)), dma((2, SUBS)),
            dma((2, SUBS)), dma((2, SUBS)),
            dma((2, Y - 1, SUBS)), dma((2, Y, SUBS)),
            dma((2,)), dma((2,)),
            dma, dma,
            dma((2, 2)), dma((2, 2)),
            dma((3,)), dma((3,)),
            dma, dma,
        ],
        compiler_params=pltpu.CompilerParams(
            collective_id=0, has_side_effects=True, vmem_limit_bytes=56 * 2**20
        ),
        cost_estimate=pl.CostEstimate(
            flops=5_000_000_000, bytes_accessed=12_000_000, transcendentals=0
        ),
    )(
        geno,
        freq.reshape(1, LOCAL),
        rhs,
        diag,
        mend.reshape(1, ROWS),
        weight.reshape(COLS, 1),
        send_rows[0],
        sire.reshape(1, ROWS),
        dam.reshape(1, ROWS),
    )
    return x_t.T, r_t.T


def solution(mesh):
    placed = (
        P("animal", "snp"),
        P("snp"),
        P("animal", None),
        P("animal", None),
        P("animal"),
        P(),
        P("animal", None, None),
        P("animal"),
        P("animal"),
    )
    return jax.shard_map(
        local,
        mesh=mesh,
        in_specs=placed,
        out_specs=(P("animal", None), P("animal", None)),
        check_vma=False,
    )
```

time: 436 us -> 144 us (0.33)
  waiting for transfers between devices: 194 us -> 0 us
  Pallas kernels: 0 us -> 137 us
  starting transfers between devices: 92.5 us -> 0 us
  other arithmetic: 65.1 us -> 0 us
  local copies, waits for them, and re-layouts: 42 us -> 5.46 us
  matrix products: 26.2 us -> 0 us
  blocking collectives: 13.5 us -> 0 us
    all_to_all x13 -> x0, waiting for transfers between devices: 194 us -> none  [the longest x7 127 us: from_everyone(): lax.all_to_all(jnp.broadcast_to(value[None], (size, *value.shape)), axis,...]
    pallas_call x0 -> x1, Pallas kernels: none -> 137 us  [local(): pl.pallas_call(kernel, out_shape=(jax.ShapeDtypeStruct((COLS, ROWS), F32)...]
    all_to_all x13 -> x0, starting transfers between devices: 92.5 us -> none  [the longest x7 43.7 us: from_everyone(): lax.all_to_all(jnp.broadcast_to(value[None], (size, *value.shape)), axis,...]
    scatter-add x6 -> x0, other arithmetic: 49.1 us -> none  [the longest x4 25.6 us: pedigree(): back.at[sire_slot].add(-0.5 * mendel_term).at[dam_slot]]
    dot_general x4 -> x0, matrix products: 26.2 us -> none  [the longest x2 14.6 us: genomic(): lax.dot_general(block, field_b, (((0,), (0,)), ((), ())), preferred_eleme...]
    gather x8 -> x0, local copies, waits for them, and re-layouts: 24 us -> none  [the longest x4 11.6 us: pedigree(): outgoing = field[outgoing_rows]]
    all_to_all x1 -> x0, blocking collectives: 13.5 us -> none  [from_everyone(): lax.all_to_all(jnp.broadcast_to(value[None], (size, *value.shape)), axis,...]
    broadcast_in_dim x8 -> x0, local copies, waits for them, and re-layouts: 9.32 us -> none  [from_everyone(): jnp.broadcast_to(value[None], (size, *value.shape))]
  transfers between devices with their start and end apart: 13 -> 0, of which waited for: 13 -> 0; matrix products, arithmetic and copies ran while one was open for 25% -> 0% of each run, Pallas kernels for 0% -> 0%
where the time goes in v1:
time: 144 us; the launch traced here: 143 us
  Pallas kernels  137 us (95%)
  local copies, waits for them, and re-layouts  5.46 us (4%)
    pallas_call x1, Pallas kernels, local(): pl.pallas_call(kernel, out_shape=(jax.ShapeDtypeStruct((COLS, ROWS), F32)...  137 us
    unnamed x2, local copies, waits for them, and re-layouts  4.07 us

profile of v1, /device:TPU:1, one launch (start us, length us, event | category | flops | bytes accessed | tf_op | source)
XLA Modules:
  0.0 143.4 jit_solution(16739894572802720748)
XLA Ops:
  0.6 1.4 copy.11.weight
  2.0 137.3 %shard_map.104 = (f32[128,1024]{1,0:T(8,128)}, f32[128,1024]{1,0:T(8,128)}) custom-call(bf16[1024,4096]{1,0:T(8,128)(2,1)} %geno.1, f32[1,4096]{1,0:T(1,128)} %bitcast.11, f32[1024,128]{1,0:T(8,128)} %rhs.1, f32[1024,128]{1,0:T(8,128)} %diag.1, f32[1,1024]{1,0:T(1,128)} %bitcast.13, f32[128,1]{1,0:T(8,128)} %copy.11.weight, s32[32,64]{1,0:T(8,128)} %bitcast.12, ...), custom_call_target="tpu_custom_call" | custom-call | flops 5000000000 | bytes 12000000 | tf_op jit(solution)/shard_map/pallas_call | solution.py:409
  139.3 2.0 %copy.12 = f32[1024,128]{1,0:T(8,128)} copy(f32[1024,128]{0,1:T(8,128)} %bitcast.9) | data formatting | bytes 1048576
  141.3 2.0 %copy.13 = f32[1024,128]{1,0:T(8,128)} copy(f32[1024,128]{0,1:T(8,128)} %bitcast.8) | data formatting | bytes 1048576

commit v2 on v1

--- a/solution.py
+++ b/solution.py
@@ -15,7 +15,7 @@
 SHARE = COLS // S
 ZSHARE = COLS // Z
 YCH = LOCAL // Y
-SUBS = 2
+SUBS = 4
 SUB = YCH // SUBS
 SLOTS = 64
 NT = (((1,), (1,)), ((), ()))
@@ -45,9 +45,10 @@
     x_out, r_out,
     block, send_hot, parent_hot, field, field_t, diag_t,
     y_own, y_send, y_recv, z_own, z_send, z_recv, effects,
-    g_own, g_send, g_recv, p_send, p_recv, p_mat, dot_send, dot_recv, final,
+    g_own, g_send, g_recv, p_send, p_recv, p_mat, dot_send, dot_recv,
+    w_full, result, scalars, norm, norm_send, norm_recv,
     load_sem, y_s, y_r, z_s, z_r, zg_s, zg_r, yg_s, yg_r, g_s, g_r, x_s, x_r,
-    p_s, p_r, d_s, d_r, f_s, f_r,
+    p_s, p_r, d_s, d_r, w_s, w_r, c_s, c_r, f_s, f_r, n_s, n_r,
 ):
     a, s = lax.axis_index("animal"), lax.axis_index("snp")
     z, y = a // Y, a % Y
@@ -76,12 +77,15 @@
     def y_lanes(which, sub):
         return pl.ds(pl.multiple_of(which * YCH + sub * SUB, SUB), SUB)
 
-    def loads(which):
-        lanes = pl.ds(pl.multiple_of(which * YCH, YCH), YCH)
-        return pltpu.make_async_copy(geno.at[:, lanes], block.at[:, lanes], load_sem.at[which])
-
-    for k in range(1, Y + 1):
-        loads((y + k) % Y).start()
+    def loads(which, sub):
+        lanes = y_lanes(which, sub)
+        return pltpu.make_async_copy(
+            geno.at[:, lanes], block.at[:, lanes], load_sem.at[which, sub]
+        )
+
+    for sub in range(SUBS):
+        for k in range(1, Y + 1):
+            loads((y + k) % Y, sub).start()
 
     barrier = pltpu.get_barrier_semaphore()
 
@@ -103,127 +107,159 @@
     z_mine = pl.ds(pl.multiple_of(z * ZSHARE, ZSHARE), ZSHARE)
     b_share = field_t[mine, :]
     d_share = diag_t[mine, :]
-    scale = weight[mine, :] * (1.0 / SNPS)
     lane = lax.broadcasted_iota(jnp.int32, (SHARE, 2 * SLOTS), 1)
+    place = lax.broadcasted_iota(jnp.int32, (SHARE, COLS), 0) + s * SHARE
+    scale = jnp.sum(
+        jnp.where(lane == place, weight[...], 0.0), axis=1, keepdims=True
+    ) * (1.0 / SNPS)
     first = lane < SLOTS
 
     pl.semaphore_wait(barrier, OWN - 1 + S - 1)
 
-    def centre(which):
-        loads(which).wait()
+    def centre(which, sub):
+        loads(which, sub).wait()
+        lanes = y_lanes(which, sub)
+        twice = 2.0 * freq[:, lanes]
 
         def rows_of(i, carry):
-            at = pl.ds(pl.multiple_of(i * 64, 64), 64)
-            lanes = pl.ds(pl.multiple_of(which * YCH, YCH), YCH)
-            block[at, lanes] = (block[at, lanes].astype(F32) - 2.0 * freq[:, lanes]).astype(BF16)
-            return carry
-
-        lax.fori_loop(0, ROWS // 64, rows_of, 0)
-
-    def effects_out(op):
+            at = pl.ds(pl.multiple_of(i * 256, 256), 256)
+            block[at, lanes] = (block[at, lanes].astype(F32) - twice).astype(BF16)
+            return carry
+
+        lax.fori_loop(0, ROWS // 256, rows_of, 0)
+
+    def spot(sub):
+        return slice(sub * SUB, (sub + 1) * SUB)
+
+    def effects_out(op, sub):
+        here = spot(sub)
+
         def one(k, carry):
             which = (y + k) % Y
             if op == 0:
-                centre(which)
-
-            def part(sub, inner):
-                here = pl.ds(pl.multiple_of(sub * SUB, SUB), SUB)
-                value = dot(field[op], block[:, y_lanes(which, sub)])
-                y_send[op, which, :, here] = value.astype(BF16)
-                remote(
-                    y_send.at[op, which, :, here], y_recv.at[op, y, :, here],
-                    y_s.at[op, k - 1, sub], y_r.at[op, y, sub], at_y(k),
-                ).start()
-                return inner
-
-            lax.fori_loop(0, SUBS, part, 0)
+                centre(which, sub)
+            value = dot(field[op], block[:, y_lanes(which, sub)])
+            y_send[op, which, :, here] = value.astype(BF16)
+            remote(
+                y_send.at[op, which, :, here], y_recv.at[op, y, :, here],
+                y_s.at[op, k - 1, sub], y_r.at[op, y, sub], at_y(k),
+            ).start()
             return carry
 
         lax.fori_loop(1, Y, one, 0)
         if op == 0:
-            centre(y)
-        for sub in range(SUBS):
-            y_own[:, sub * SUB : (sub + 1) * SUB] = dot(field[op], block[:, y_lanes(y, sub)])
-
-    def effects_mid(op):
-        for sub in range(SUBS):
-            here = slice(sub * SUB, (sub + 1) * SUB)
-            total = y_own[:, here]
-            for k in range(1, Y):
-                which = (y + k) % Y
-                piece = y_recv.at[op, which, :, here]
-                settle(piece, y_s.at[op, k - 1, sub], y_r.at[op, which, sub], at_y(k)).wait_recv()
-                total = total + piece[...].astype(F32)
-            z_own[:, here] = total
-            z_send[op, :, here] = total.astype(BF16)
-
-            def give(k, carry):
-                peer_rows = pl.ds(pl.multiple_of(((z + k) % Z) * ZSHARE, ZSHARE), ZSHARE)
-                remote(
-                    z_send.at[op, peer_rows, here], z_recv.at[op, z, :, here],
-                    z_s.at[op, sub], z_r.at[op, sub], at_z(k),
-                ).start()
-                return carry
-
-            lax.fori_loop(1, Z, give, 0)
-
-    def effects_sum(op):
-        for sub in range(SUBS):
-            here = slice(sub * SUB, (sub + 1) * SUB)
-            settle(
-                z_recv.at[op, 0 : Z - 1, :, here], z_s.at[op, sub], z_r.at[op, sub], at_z(1)
-            ).wait_recv()
-            total = z_own[z_mine, here]
-            for k in range(1, Z):
-                total = total + z_recv[op, (z + k) % Z, :, here].astype(F32)
-            effects[op, z_mine, y_lanes(y, sub)] = total.astype(BF16)
-
-            def give(k, carry):
-                piece = effects.at[op, z_mine, y_lanes(y, sub)]
-                remote(piece, piece, zg_s.at[op, sub], zg_r.at[op, sub], at_z(k)).start()
-                return carry
-
-            lax.fori_loop(1, Z, give, 0)
-
-    def effects_spread(op):
-        for sub in range(SUBS):
-            settle(
-                effects.at[op, 0 : COLS - ZSHARE, y_lanes(y, sub)],
-                zg_s.at[op, sub], zg_r.at[op, sub], at_z(1),
-            ).wait_recv()
-            for k in range(1, Y):
-                piece = effects.at[op, :, y_lanes(y, sub)]
-                remote(
-                    piece, piece, yg_s.at[op, k - 1, sub], yg_r.at[op, y, sub], at_y(k)
-                ).start()
-
-    def genomic_own(op):
-        lanes = pl.ds(pl.multiple_of(y * YCH, YCH), YCH)
-        g_own[...] = dot_nt(effects[op, :, lanes], block[:, lanes])
+            centre(y, sub)
+        y_own[:, here] = dot(field[op], block[:, y_lanes(y, sub)])
+
+    def effects_mid(op, sub):
+        here = spot(sub)
+        total = y_own[:, here]
+        for k in range(1, Y):
+            which = (y + k) % Y
+            piece = y_recv.at[op, which, :, here]
+            settle(piece, y_s.at[op, k - 1, sub], y_r.at[op, which, sub], at_y(k)).wait_recv()
+            total = total + piece[...].astype(F32)
+        z_own[:, here] = total
+        z_send[op, :, here] = total.astype(BF16)
+
+        def give(k, carry):
+            peer_rows = pl.ds(pl.multiple_of(((z + k) % Z) * ZSHARE, ZSHARE), ZSHARE)
+            remote(
+                z_send.at[op, peer_rows, here], z_recv.at[op, z, :, here],
+                z_s.at[op, sub], z_r.at[op, sub], at_z(k),
+            ).start()
+            return carry
+
+        lax.fori_loop(1, Z, give, 0)
+
+    def effects_sum(op, sub):
+        here = spot(sub)
+        settle(
+            z_recv.at[op, 0 : Z - 1, :, here], z_s.at[op, sub], z_r.at[op, sub], at_z(1)
+        ).wait_recv()
+        total = z_own[z_mine, here]
+        for k in range(1, Z):
+            total = total + z_recv[op, (z + k) % Z, :, here].astype(F32)
+        effects[op, z_mine, y_lanes(y, sub)] = total.astype(BF16)
+
+        def give(k, carry):
+            piece = effects.at[op, z_mine, y_lanes(y, sub)]
+            remote(piece, piece, zg_s.at[op, sub], zg_r.at[op, sub], at_z(k)).start()
+            return carry
+
+        lax.fori_loop(1, Z, give, 0)
+
+    def take(op, lanes, fresh):
+        piece = effects[op, :, lanes]
+        value = dot_nt(piece, block[:, lanes])
+        if fresh:
+            g_own[...] = value
+        else:
+            g_own[...] += value
+        if op == 1:
+            wide = piece.astype(F32)
+            square = jnp.zeros((COLS, 128), F32)
+            for part in range(SUB // 128):
+                one = wide[:, part * 128 : (part + 1) * 128]
+                square = square + one * one
+            if fresh:
+                norm[...] = square
+            else:
+                norm[...] += square
+
+    def effects_spread(op, sub):
+        lanes = y_lanes(y, sub)
+        settle(
+            effects.at[op, 0 : COLS - ZSHARE, lanes], zg_s.at[op, sub], zg_r.at[op, sub], at_z(1)
+        ).wait_recv()
+        for k in range(1, Y):
+            piece = effects.at[op, :, lanes]
+            remote(piece, piece, yg_s.at[op, k - 1, sub], yg_r.at[op, y, sub], at_y(k)).start()
+        take(op, lanes, sub == 0)
 
     def genomic(op):
         for sub in range(SUBS):
-            for k in range(1, Y):
+            def one(k, carry):
                 which = (y + k) % Y
                 lanes = y_lanes(which, sub)
-                piece = effects.at[op, :, lanes]
-                settle(piece, yg_s.at[op, k - 1, sub], yg_r.at[op, which, sub], at_y(k)).wait_recv()
-                g_own[...] += dot_nt(piece[...], block[:, lanes])
+                settle(
+                    effects.at[op, :, lanes],
+                    yg_s.at[op, k - 1, sub], yg_r.at[op, which, sub], at_y(k),
+                ).wait_recv()
+                take(op, lanes, False)
+                return carry
+
+            lax.fori_loop(1, Y, one, 0)
         g_send[op] = g_own[...].astype(BF16)
+        if op == 1:
+            norm_send[...] = jnp.broadcast_to(
+                jnp.sum(norm[...], axis=1, keepdims=True), (COLS, 128)
+            )
 
         def give(k, carry):
             peer_rows = pl.ds(pl.multiple_of(((s + k) % S) * SHARE, SHARE), SHARE)
+            if op == 1:
+                remote(norm_send.at[peer_rows, :], norm_recv.at[s], n_s, n_r, at_s(k)).start()
             remote(
                 g_send.at[op, peer_rows, :], g_recv.at[op, s], g_s.at[op], g_r.at[op], at_s(k)
             ).start()
             return carry
 
         lax.fori_loop(1, S, give, 0)
+
+    def genomic_in(op):
         settle(g_recv.at[op, 0 : S - 1], g_s.at[op], g_r.at[op], at_s(1)).wait_recv()
         total = g_own[mine, :]
         for k in range(1, S):
             total = total + g_recv[op, (s + k) % S].astype(F32)
         return total
+
+    def norm_in():
+        settle(norm_recv.at[0 : S - 1], n_s, n_r, at_s(1)).wait_recv()
+        total = norm_send[mine, :]
+        for k in range(1, S):
+            total = total + norm_recv[(s + k) % S]
+        return total[:, 0:1]
 
     def relay_out(leg, op, value):
         both = value
@@ -283,10 +319,11 @@
     def pedigree_mid(op, value):
         parents = fold(dot(relay_in(0, op), parent_hot[...]))
         term = mend[...] * (value - 0.5 * parents)
+        form = term * (value - 0.5 * parents)
         back = -0.5 * fold(dot_nt(halves(term), parent_hot[...]))
         high = back.astype(BF16).astype(F32)
         relay_out(1, op, jnp.concatenate([high, back - high], axis=0))
-        return term
+        return term, form
 
     def pedigree_end(op, term):
         return term + fold(dot_nt(relay_in(1, op), send_hot[...]))
@@ -304,13 +341,14 @@
     def field_arrives():
         settle(field.at[1, 0 : COLS - SHARE, :], x_s, x_r, at_s(1)).wait_recv()
 
-    def dots_out(batch, one, two):
-        tile = jnp.where(
-            lane == 0,
-            jnp.sum(one, axis=1, keepdims=True),
-            jnp.where(lane == 1, jnp.sum(two, axis=1, keepdims=True), 0.0),
-        )
-        dot_send[batch] = tile
+    def pack(*columns):
+        tile = jnp.zeros((SHARE, 128), F32)
+        for position, column in enumerate(columns):
+            tile = jnp.where(lane == position, column, tile)
+        return tile
+
+    def dots_out(batch, *products):
+        dot_send[batch] = pack(*[jnp.sum(p, axis=1, keepdims=True) for p in products])
 
         def give(k, carry):
             remote(
@@ -324,58 +362,96 @@
         settle(dot_recv.at[batch, 0 : OWN - 1], d_s.at[batch], d_r.at[batch], at_a(1)).wait_recv()
         dot_recv[batch, a] = dot_send[batch]
         total = jnp.sum(dot_recv[batch], axis=0)
-        return total[:, 0:1], total[:, 1:2]
-
-    effects_out(0)
+        return total[:, 0:1], total[:, 1:2], total[:, 2:3]
+
+    def to_snp(ref, send_sem, recv_sem):
+        def give(k, carry):
+            piece = ref.at[mine, :]
+            remote(piece, piece, send_sem, recv_sem, at_s(k)).start()
+            return carry
+
+        lax.fori_loop(1, S, give, 0)
+
+    def all_of(ref, send_sem, recv_sem):
+        return settle(ref.at[0 : COLS - SHARE, :], send_sem, recv_sem, at_s(1))
+
+    effects_out(0, 0)
+    effects_out(0, 1)
+    effects_out(0, 2)
+    effects_mid(0, 0)
+    effects_out(0, 3)
+    effects_mid(0, 1)
     make_send_hot()
     pedigree_out(0, b_share)
+    effects_mid(0, 2)
+    effects_sum(0, 0)
+    effects_mid(0, 3)
+    effects_sum(0, 1)
     make_parent_hot()
-    effects_mid(0)
-    term = pedigree_mid(0, b_share)
-    effects_sum(0)
-    effects_spread(0)
-    genomic_own(0)
+    effects_sum(0, 2)
+    effects_spread(0, 0)
+    effects_sum(0, 3)
+    effects_spread(0, 1)
+    term, _ = pedigree_mid(0, b_share)
+    effects_spread(0, 2)
+    effects_spread(0, 3)
     ped = pedigree_end(0, term)
-    w_share = d_share * b_share + ped + scale * genomic(0)
+    genomic(0)
+    w_share = d_share * b_share + ped + scale * genomic_in(0)
     share_field(w_share)
-    dots_out(0, b_share * b_share, w_share * b_share)
     pedigree_out(1, w_share)
+    dots_out(0, b_share * b_share, w_share * b_share, w_share * w_share)
+    w_full[mine, :] = w_share
     field_arrives()
 
-    effects_out(1)
-    gamma0, delta0 = dots_in(0)
+    effects_out(1, 0)
+    effects_out(1, 1)
+    to_snp(w_full, w_s, w_r)
+    effects_out(1, 2)
+    effects_mid(1, 0)
+    effects_out(1, 3)
+    effects_mid(1, 1)
+    term, form = pedigree_mid(1, w_share)
+    effects_mid(1, 2)
+    effects_sum(1, 0)
+    effects_mid(1, 3)
+    effects_sum(1, 1)
+    gamma0, delta0, square0 = dots_in(0)
     alpha0 = gamma0 / delta0
     r_share = b_share - alpha0 * w_share
-    dots_out(1, r_share * r_share, r_share * w_share)
-    term = pedigree_mid(1, w_share)
-    effects_mid(1)
-    effects_sum(1)
-    effects_spread(1)
-    genomic_own(1)
+    dots_out(1, r_share * r_share, r_share * w_share, d_share * w_share * w_share + form)
+    effects_sum(1, 2)
+    effects_spread(1, 0)
+    effects_sum(1, 3)
+    effects_spread(1, 1)
+    effects_spread(1, 2)
+    effects_spread(1, 3)
     ped = pedigree_end(1, term)
-    gamma1, _ = dots_in(1)
-    q_share = d_share * w_share + ped + scale * genomic(1)
+    gamma1, cross, quad = dots_in(1)
+    beta = gamma1 / gamma0
+    genomic(1)
+    quad = quad + scale * norm_in()
+    delta1 = cross - alpha0 * (square0 - alpha0 * quad)
+    alpha1 = gamma1 / (delta1 - beta * gamma1 / alpha0)
+    scalars[mine, :] = pack(alpha0, beta, alpha1)
+    to_snp(scalars, c_s, c_r)
+    q_share = d_share * w_share + ped + scale * genomic_in(1)
     w1_share = w_share - alpha0 * q_share
-    dots_out(2, w1_share * r_share, w1_share)
-    delta1, _ = dots_in(2)
-    beta = gamma1 / gamma0
-    alpha1 = gamma1 / (delta1 - beta * gamma1 / alpha0)
-    final[0, mine, :] = alpha0 * b_share + alpha1 * (r_share + beta * b_share)
-    final[1, mine, :] = r_share - alpha1 * (w1_share + beta * w_share)
-
-    def give(k, carry):
-        piece = final.at[:, mine, :]
-        remote(piece, piece, f_s, f_r, at_s(k)).start()
-        return carry
-
-    lax.fori_loop(1, S, give, 0)
-    settle(final.at[:, 0 : COLS - SHARE, :], f_s, f_r, at_s(1)).wait()
-    x_out[...] = final[0]
-    r_out[...] = final[1]
+    result[mine, :] = (r_share - alpha1 * (w1_share + beta * w_share)).astype(BF16)
+    to_snp(result, f_s, f_r)
+    all_of(w_full, w_s, w_r).wait()
+    all_of(scalars, c_s, c_r).wait()
+    alpha0, beta, alpha1 = (scalars[:, i : i + 1] for i in range(3))
+    b_full = field_t[...]
+    x_out[...] = (
+        alpha0 * b_full + alpha1 * ((b_full - alpha0 * w_full[...]) + beta * b_full)
+    ).T
+    all_of(result, f_s, f_r).wait()
+    r_out[...] = result[...].astype(F32).T
 
     for op in range(2):
         for sub in range(SUBS):
-            here = slice(sub * SUB, (sub + 1) * SUB)
+            here = spot(sub)
             for k in range(1, Y):
                 settle(
                     y_send.at[op, 0, :, here], y_s.at[op, k - 1, sub], y_r.at[op, 0, sub], at_y(k)
@@ -397,7 +473,8 @@
                 p_recv.at[op, leg, 0 : OWN - 1], p_s.at[op, leg], p_r.at[op, leg], at_a(1)
             ).wait_send()
     settle(field.at[1, 0 : COLS - SHARE, :], x_s, x_r, at_s(1)).wait_send()
-    for batch in range(3):
+    settle(norm_recv.at[0 : S - 1], n_s, n_r, at_s(1)).wait_send()
+    for batch in range(2):
         settle(
             dot_recv.at[batch, 0 : OWN - 1], d_s.at[batch], d_r.at[batch], at_a(1)
         ).wait_send()
@@ -406,9 +483,9 @@
 def local(geno, freq, rhs, diag, mend, weight, send_rows, sire, dam):
     vmem = pl.BlockSpec(memory_space=pltpu.VMEM)
     dma = pltpu.SemaphoreType.DMA
-    x_t, r_t = pl.pallas_call(
+    return pl.pallas_call(
         kernel,
-        out_shape=(jax.ShapeDtypeStruct((COLS, ROWS), F32),) * 2,
+        out_shape=(jax.ShapeDtypeStruct((ROWS, COLS), F32),) * 2,
         in_specs=[pl.BlockSpec(memory_space=pl.ANY)] + [vmem] * 8,
         out_specs=(vmem, vmem),
         scratch_shapes=[
@@ -431,10 +508,15 @@
             pltpu.VMEM((2, 2, OWN, SHARE, 2 * SLOTS), BF16),
             pltpu.VMEM((2, 2, OWN, SHARE, 2 * SLOTS), BF16),
             pltpu.VMEM((2 * SHARE, OWN * SLOTS), BF16),
-            pltpu.VMEM((3, SHARE, 128), F32),
-            pltpu.VMEM((3, OWN, SHARE, 128), F32),
-            pltpu.VMEM((2, COLS, ROWS), F32),
-            dma((Y,)),
+            pltpu.VMEM((2, SHARE, 128), F32),
+            pltpu.VMEM((2, OWN, SHARE, 128), F32),
+            pltpu.VMEM((COLS, ROWS), F32),
+            pltpu.VMEM((COLS, ROWS), BF16),
+            pltpu.VMEM((COLS, 128), F32),
+            pltpu.VMEM((COLS, 128), F32),
+            pltpu.VMEM((COLS, 128), F32),
+            pltpu.VMEM((S, SHARE, 128), F32),
+            dma((Y, SUBS)),
             dma((2, Y - 1, SUBS)), dma((2, Y, SUBS)),
             dma((2, SUBS)), dma((2, SUBS)),
             dma((2, SUBS)), dma((2, SUBS)),
@@ -442,7 +524,10 @@
             dma((2,)), dma((2,)),
             dma, dma,
             dma((2, 2)), dma((2, 2)),
-            dma((3,)), dma((3,)),
+            dma((2,)), dma((2,)),
+            dma, dma,
+            dma, dma,
+            dma, dma,
             dma, dma,
         ],
         compiler_params=pltpu.CompilerParams(
@@ -457,12 +542,11 @@
         rhs,
         diag,
         mend.reshape(1, ROWS),
-        weight.reshape(COLS, 1),
+        weight.reshape(1, COLS),
         send_rows[0],
         sire.reshape(1, ROWS),
         dam.reshape(1, ROWS),
     )
-    return x_t.T, r_t.T
 
 
 def solution(mesh):

time: 144 us -> 120 us (0.83)
  Pallas kernels: 137 us -> 115 us
  local copies, waits for them, and re-layouts: 5.46 us -> 3.74 us
    pallas_call x1, Pallas kernels: 137 us -> 115 us  [local(): pl.pallas_call(kernel, out_shape=(jax.ShapeDtypeStruct((ROWS, COLS), F32)...]
where the time goes in v2:
time: 120 us
  Pallas kernels  115 us (96%)
  local copies, waits for them, and re-layouts  3.74 us (3%)
    pallas_call x1, Pallas kernels, local(): pl.pallas_call(kernel, out_shape=(jax.ShapeDtypeStruct((ROWS, COLS), F32)...  115 us
    unnamed x2, local copies, waits for them, and re-layouts  3.74 us

profile of v2, /device:TPU:1, one launch (start us, length us, event | category | flops | bytes accessed | tf_op | source)
XLA Modules:
  0.0 119.6 jit_solution(4333316530036100892)
XLA Ops:
  0.6 115.2 %shard_map.104 = (f32[1024,128]{1,0:T(8,128)}, f32[1024,128]{1,0:T(8,128)}) custom-call(bf16[1024,4096]{1,0:T(8,128)(2,1)} %geno.1, f32[1,4096]{1,0:T(1,128)} %bitcast.6, f32[1024,128]{1,0:T(8,128)} %rhs.1, f32[1024,128]{1,0:T(8,128)} %diag.1, f32[1,1024]{1,0:T(1,128)} %bitcast.8, f32[1,128]{1,0:T(1,128)} %bitcast.11, s32[32,64]{1,0:T(8,128)} %bitcast.7, ...), custom_call_target="tpu_custom_call" | custom-call | flops 5000000000 | bytes 12000000 | tf_op jit(solution)/shard_map/pallas_call | solution.py:486
  115.8 1.9 %copy.13 = f32[1024,128]{1,0:T(8,128)} copy(f32[1024,128]{1,0:T(8,128)} %get-tuple-element.4) | data formatting | bytes 1048576
  117.7 1.9 %copy.14 = f32[1024,128]{1,0:T(8,128)} copy(f32[1024,128]{1,0:T(8,128)} %get-tuple-element.5) | data formatting | bytes 1048576

commit v3 on v2

--- a/solution.py
+++ b/solution.py
@@ -18,6 +18,7 @@
 SUBS = 4
 SUB = YCH // SUBS
 SLOTS = 64
+PARTS = 3
 NT = (((1,), (1,)), ((), ()))
 F32, BF16 = jnp.float32, jnp.bfloat16
 
@@ -45,10 +46,10 @@
     x_out, r_out,
     block, send_hot, parent_hot, field, field_t, diag_t,
     y_own, y_send, y_recv, z_own, z_send, z_recv, effects,
-    g_own, g_send, g_recv, p_send, p_recv, p_mat, dot_send, dot_recv,
+    g_own, g_send, g_recv, p_send, p_recv, p_mat,
     w_full, result, scalars, norm, norm_send, norm_recv,
     load_sem, y_s, y_r, z_s, z_r, zg_s, zg_r, yg_s, yg_r, g_s, g_r, x_s, x_r,
-    p_s, p_r, d_s, d_r, w_s, w_r, c_s, c_r, f_s, f_r, n_s, n_r,
+    p_s, p_r, w_s, w_r, c_s, c_r, f_s, f_r, n_s, n_r,
 ):
     a, s = lax.axis_index("animal"), lax.axis_index("snp")
     z, y = a // Y, a % Y
@@ -75,17 +76,18 @@
         return remote(ref, ref, send_sem, recv_sem, peer)
 
     def y_lanes(which, sub):
-        return pl.ds(pl.multiple_of(which * YCH + sub * SUB, SUB), SUB)
-
-    def loads(which, sub):
-        lanes = y_lanes(which, sub)
+        return pl.ds(pl.multiple_of(sub * YCH + which * SUB, SUB), SUB)
+
+    def chunk(sub):
+        return slice(sub * YCH, (sub + 1) * YCH)
+
+    def loads(sub):
         return pltpu.make_async_copy(
-            geno.at[:, lanes], block.at[:, lanes], load_sem.at[which, sub]
+            geno.at[:, chunk(sub)], block.at[:, chunk(sub)], load_sem.at[sub]
         )
 
     for sub in range(SUBS):
-        for k in range(1, Y + 1):
-            loads((y + k) % Y, sub).start()
+        loads(sub).start()
 
     barrier = pltpu.get_barrier_semaphore()
 
@@ -101,12 +103,10 @@
     lax.fori_loop(1, S, greet_s, 0)
 
     field_t[...] = rhs[...].T
-    diag_t[...] = diag[...].T
     field[0] = field_t[...].astype(BF16)
     mine = pl.ds(pl.multiple_of(s * SHARE, SHARE), SHARE)
     z_mine = pl.ds(pl.multiple_of(z * ZSHARE, ZSHARE), ZSHARE)
     b_share = field_t[mine, :]
-    d_share = diag_t[mine, :]
     lane = lax.broadcasted_iota(jnp.int32, (SHARE, 2 * SLOTS), 1)
     place = lax.broadcasted_iota(jnp.int32, (SHARE, COLS), 0) + s * SHARE
     scale = jnp.sum(
@@ -114,46 +114,40 @@
     ) * (1.0 / SNPS)
     first = lane < SLOTS
 
-    pl.semaphore_wait(barrier, OWN - 1 + S - 1)
-
-    def centre(which, sub):
-        loads(which, sub).wait()
-        lanes = y_lanes(which, sub)
+    def centre(sub):
+        loads(sub).wait()
+        lanes = chunk(sub)
         twice = 2.0 * freq[:, lanes]
 
         def rows_of(i, carry):
-            at = pl.ds(pl.multiple_of(i * 256, 256), 256)
+            at = pl.ds(pl.multiple_of(i * 128, 128), 128)
             block[at, lanes] = (block[at, lanes].astype(F32) - twice).astype(BF16)
             return carry
 
-        lax.fori_loop(0, ROWS // 256, rows_of, 0)
+        lax.fori_loop(0, ROWS // 128, rows_of, 0)
 
     def spot(sub):
         return slice(sub * SUB, (sub + 1) * SUB)
 
-    def effects_out(op, sub):
-        here = spot(sub)
-
-        def one(k, carry):
-            which = (y + k) % Y
-            if op == 0:
-                centre(which, sub)
-            value = dot(field[op], block[:, y_lanes(which, sub)])
-            y_send[op, which, :, here] = value.astype(BF16)
+    def effects_send(op, sub):
+        for k in range(1, Y):
             remote(
-                y_send.at[op, which, :, here], y_recv.at[op, y, :, here],
+                y_send.at[op, :, y_lanes((y + k) % Y, sub)], y_recv.at[op, y, :, spot(sub)],
                 y_s.at[op, k - 1, sub], y_r.at[op, y, sub], at_y(k),
             ).start()
-            return carry
-
-        lax.fori_loop(1, Y, one, 0)
+
+    def effects_out(op, sub, send=True):
         if op == 0:
-            centre(y, sub)
-        y_own[:, here] = dot(field[op], block[:, y_lanes(y, sub)])
+            centre(sub)
+        value = dot(field[op], block[:, chunk(sub)])
+        y_send[op, :, chunk(sub)] = value.astype(BF16)
+        if send:
+            effects_send(op, sub)
+        y_own[:, chunk(sub)] = value
 
     def effects_mid(op, sub):
         here = spot(sub)
-        total = y_own[:, here]
+        total = y_own[:, y_lanes(y, sub)]
         for k in range(1, Y):
             which = (y + k) % Y
             piece = y_recv.at[op, which, :, here]
@@ -189,24 +183,6 @@
 
         lax.fori_loop(1, Z, give, 0)
 
-    def take(op, lanes, fresh):
-        piece = effects[op, :, lanes]
-        value = dot_nt(piece, block[:, lanes])
-        if fresh:
-            g_own[...] = value
-        else:
-            g_own[...] += value
-        if op == 1:
-            wide = piece.astype(F32)
-            square = jnp.zeros((COLS, 128), F32)
-            for part in range(SUB // 128):
-                one = wide[:, part * 128 : (part + 1) * 128]
-                square = square + one * one
-            if fresh:
-                norm[...] = square
-            else:
-                norm[...] += square
-
     def effects_spread(op, sub):
         lanes = y_lanes(y, sub)
         settle(
@@ -215,21 +191,31 @@
         for k in range(1, Y):
             piece = effects.at[op, :, lanes]
             remote(piece, piece, yg_s.at[op, k - 1, sub], yg_r.at[op, y, sub], at_y(k)).start()
-        take(op, lanes, sub == 0)
-
-    def genomic(op):
-        for sub in range(SUBS):
-            def one(k, carry):
-                which = (y + k) % Y
-                lanes = y_lanes(which, sub)
-                settle(
-                    effects.at[op, :, lanes],
-                    yg_s.at[op, k - 1, sub], yg_r.at[op, which, sub], at_y(k),
-                ).wait_recv()
-                take(op, lanes, False)
-                return carry
-
-            lax.fori_loop(1, Y, one, 0)
+
+    def take(op, sub):
+        for k in range(1, Y):
+            which = (y + k) % Y
+            settle(
+                effects.at[op, :, y_lanes(which, sub)],
+                yg_s.at[op, k - 1, sub], yg_r.at[op, which, sub], at_y(k),
+            ).wait_recv()
+        piece = effects[op, :, chunk(sub)]
+        value = dot_nt(piece, block[:, chunk(sub)])
+        if sub == 0:
+            g_own[...] = value
+        else:
+            g_own[...] += value
+        if op == 1:
+            square = jnp.zeros((COLS, 128), F32)
+            for part in range(YCH // 128):
+                one = piece[:, part * 128 : (part + 1) * 128].astype(F32)
+                square = square + one * one
+            if sub == 0:
+                norm[...] = square
+            else:
+                norm[...] += square
+
+    def genomic_out(op):
         g_send[op] = g_own[...].astype(BF16)
         if op == 1:
             norm_send[...] = jnp.broadcast_to(
@@ -261,18 +247,37 @@
             total = total + norm_recv[(s + k) % S]
         return total[:, 0:1]
 
-    def relay_out(leg, op, value):
-        both = value
+    def pack(*columns):
+        tile = jnp.zeros((SHARE, 128), F32)
+        for position, column in enumerate(columns):
+            tile = jnp.where(lane == position, column, tile)
+        return tile
+
+    def depth(op):
+        return 2 * SHARE if op == 1 else SHARE
+
+    def relay_out(leg, op, both, products=()):
         for pair in range(OWN // 2):
             lanes = slice(pair * 2 * SLOTS, (pair + 1) * 2 * SLOTS)
             high, low = both[:SHARE, lanes], both[SHARE:, lanes]
-            p_send[op, leg, 2 * pair] = jnp.where(first, high, swap(low)).astype(BF16)
-            p_send[op, leg, 2 * pair + 1] = jnp.where(first, swap(high), low).astype(BF16)
+            p_send[op, leg, 2 * pair, :SHARE] = jnp.where(first, high, swap(low)).astype(BF16)
+            p_send[op, leg, 2 * pair + 1, :SHARE] = jnp.where(first, swap(high), low).astype(BF16)
+        if products:
+            parts = []
+            for product in products:
+                left = jnp.sum(product, axis=1, keepdims=True)
+                for _ in range(PARTS):
+                    part = left.astype(BF16).astype(F32)
+                    left = left - part
+                    parts.append(part)
+            tile = pack(*parts).astype(BF16)
+            for peer in range(OWN):
+                p_send[op, leg, peer, SHARE:] = tile
 
         def give(k, carry):
             peer = (a + k) % OWN
             remote(
-                p_send.at[op, leg, peer], p_recv.at[op, leg, a],
+                p_send.at[op, leg, peer, 0 : depth(op)], p_recv.at[op, leg, a, 0 : depth(op)],
                 p_s.at[op, leg], p_r.at[op, leg], at_a(k),
             ).start()
             return carry
@@ -281,16 +286,23 @@
 
     def relay_in(leg, op):
         settle(
-            p_recv.at[op, leg, 0 : OWN - 1], p_s.at[op, leg], p_r.at[op, leg], at_a(1)
+            p_recv.at[op, leg, 0 : OWN - 1, 0 : depth(op)],
+            p_s.at[op, leg], p_r.at[op, leg], at_a(1),
         ).wait_recv()
         p_recv[op, leg, a] = p_send[op, leg, a]
         for pair in range(OWN // 2):
             lanes = slice(pair * 2 * SLOTS, (pair + 1) * 2 * SLOTS)
-            one = p_recv[op, leg, 2 * pair].astype(F32)
-            two = p_recv[op, leg, 2 * pair + 1].astype(F32)
+            one = p_recv[op, leg, 2 * pair, :SHARE].astype(F32)
+            two = p_recv[op, leg, 2 * pair + 1, :SHARE].astype(F32)
             p_mat[:SHARE, lanes] = jnp.where(first, one, swap(two)).astype(BF16)
             p_mat[SHARE:, lanes] = jnp.where(first, swap(one), two).astype(BF16)
         return p_mat[...]
+
+    def totals(leg):
+        tile = jnp.sum(p_recv[1, leg, :, SHARE:, :].astype(F32), axis=0)
+        return tuple(
+            jnp.sum(tile[:, i * PARTS : (i + 1) * PARTS], axis=1, keepdims=True) for i in range(3)
+        )
 
     def fold(both):
         return both[:SHARE] + both[SHARE:]
@@ -313,17 +325,28 @@
 
         lax.fori_loop(0, OWN * SLOTS // 128, some, 0)
 
-    def pedigree_out(op, value):
-        relay_out(0, op, dot(halves(value), send_hot[...]))
+    def pedigree_out(op, value, products=()):
+        relay_out(0, op, dot(halves(value), send_hot[...]), products)
 
     def pedigree_mid(op, value):
         parents = fold(dot(relay_in(0, op), parent_hot[...]))
-        term = mend[...] * (value - 0.5 * parents)
-        form = term * (value - 0.5 * parents)
+        lacks = value - 0.5 * parents
+        return lacks, mend[...] * lacks
+
+    def pedigree_back(op, value, lacks, term):
         back = -0.5 * fold(dot_nt(halves(term), parent_hot[...]))
         high = back.astype(BF16).astype(F32)
-        relay_out(1, op, jnp.concatenate([high, back - high], axis=0))
-        return term, form
+        both = jnp.concatenate([high, back - high], axis=0)
+        if op == 0:
+            relay_out(1, op, both)
+            return ()
+        gamma, delta, square = totals(0)
+        alpha = gamma / delta
+        rest = b_share - alpha * value
+        relay_out(
+            1, op, both, (rest * rest, rest * value, d_share * value * value + term * lacks)
+        )
+        return gamma, alpha, square, rest
 
     def pedigree_end(op, term):
         return term + fold(dot_nt(relay_in(1, op), send_hot[...]))
@@ -340,29 +363,6 @@
 
     def field_arrives():
         settle(field.at[1, 0 : COLS - SHARE, :], x_s, x_r, at_s(1)).wait_recv()
-
-    def pack(*columns):
-        tile = jnp.zeros((SHARE, 128), F32)
-        for position, column in enumerate(columns):
-            tile = jnp.where(lane == position, column, tile)
-        return tile
-
-    def dots_out(batch, *products):
-        dot_send[batch] = pack(*[jnp.sum(p, axis=1, keepdims=True) for p in products])
-
-        def give(k, carry):
-            remote(
-                dot_send.at[batch], dot_recv.at[batch, a], d_s.at[batch], d_r.at[batch], at_a(k)
-            ).start()
-            return carry
-
-        lax.fori_loop(1, OWN, give, 0)
-
-    def dots_in(batch):
-        settle(dot_recv.at[batch, 0 : OWN - 1], d_s.at[batch], d_r.at[batch], at_a(1)).wait_recv()
-        dot_recv[batch, a] = dot_send[batch]
-        total = jnp.sum(dot_recv[batch], axis=0)
-        return total[:, 0:1], total[:, 1:2], total[:, 2:3]
 
     def to_snp(ref, send_sem, recv_sem):
         def give(k, carry):
@@ -375,61 +375,72 @@
     def all_of(ref, send_sem, recv_sem):
         return settle(ref.at[0 : COLS - SHARE, :], send_sem, recv_sem, at_s(1))
 
-    effects_out(0, 0)
-    effects_out(0, 1)
+    effects_out(0, 0, send=False)
+    effects_out(0, 1, send=False)
+    make_send_hot()
+    pl.semaphore_wait(barrier, OWN - 1 + S - 1)
+    effects_send(0, 0)
+    effects_send(0, 1)
     effects_out(0, 2)
+    effects_out(0, 3)
+    pedigree_out(0, b_share)
+    make_parent_hot()
+    diag_t[...] = diag[...].T
+    d_share = diag_t[mine, :]
     effects_mid(0, 0)
-    effects_out(0, 3)
     effects_mid(0, 1)
-    make_send_hot()
-    pedigree_out(0, b_share)
     effects_mid(0, 2)
     effects_sum(0, 0)
     effects_mid(0, 3)
     effects_sum(0, 1)
-    make_parent_hot()
+    lacks, term = pedigree_mid(0, b_share)
+    effects_spread(0, 0)
+    pedigree_back(0, b_share, lacks, term)
     effects_sum(0, 2)
-    effects_spread(0, 0)
+    effects_spread(0, 1)
     effects_sum(0, 3)
-    effects_spread(0, 1)
-    term, _ = pedigree_mid(0, b_share)
     effects_spread(0, 2)
+    take(0, 0)
     effects_spread(0, 3)
+    take(0, 1)
+    take(0, 2)
     ped = pedigree_end(0, term)
-    genomic(0)
-    w_share = d_share * b_share + ped + scale * genomic_in(0)
+    take(0, 3)
+    genomic_out(0)
+    w_share = d_share * b_share + ped
+    w_share = w_share + scale * genomic_in(0)
     share_field(w_share)
-    pedigree_out(1, w_share)
-    dots_out(0, b_share * b_share, w_share * b_share, w_share * w_share)
+    pedigree_out(1, w_share, (b_share * b_share, w_share * b_share, w_share * w_share))
     w_full[mine, :] = w_share
     field_arrives()
 
     effects_out(1, 0)
     effects_out(1, 1)
+    effects_out(1, 2)
+    effects_out(1, 3)
     to_snp(w_full, w_s, w_r)
-    effects_out(1, 2)
+    lacks, term = pedigree_mid(1, w_share)
     effects_mid(1, 0)
-    effects_out(1, 3)
+    gamma0, alpha0, square0, r_share = pedigree_back(1, w_share, lacks, term)
     effects_mid(1, 1)
-    term, form = pedigree_mid(1, w_share)
     effects_mid(1, 2)
     effects_sum(1, 0)
     effects_mid(1, 3)
     effects_sum(1, 1)
-    gamma0, delta0, square0 = dots_in(0)
-    alpha0 = gamma0 / delta0
-    r_share = b_share - alpha0 * w_share
-    dots_out(1, r_share * r_share, r_share * w_share, d_share * w_share * w_share + form)
+    effects_spread(1, 0)
     effects_sum(1, 2)
-    effects_spread(1, 0)
+    effects_spread(1, 1)
     effects_sum(1, 3)
-    effects_spread(1, 1)
+    ped = pedigree_end(1, term)
     effects_spread(1, 2)
+    take(1, 0)
     effects_spread(1, 3)
-    ped = pedigree_end(1, term)
-    gamma1, cross, quad = dots_in(1)
+    take(1, 1)
+    take(1, 2)
+    gamma1, cross, quad = totals(1)
     beta = gamma1 / gamma0
-    genomic(1)
+    take(1, 3)
+    genomic_out(1)
     quad = quad + scale * norm_in()
     delta1 = cross - alpha0 * (square0 - alpha0 * quad)
     alpha1 = gamma1 / (delta1 - beta * gamma1 / alpha0)
@@ -454,7 +465,7 @@
             here = spot(sub)
             for k in range(1, Y):
                 settle(
-                    y_send.at[op, 0, :, here], y_s.at[op, k - 1, sub], y_r.at[op, 0, sub], at_y(k)
+                    y_send.at[op, :, y_lanes(0, sub)], y_s.at[op, k - 1, sub], y_r.at[op, 0, sub], at_y(k)
                 ).wait_send()
                 settle(
                     effects.at[op, :, y_lanes(y, sub)],
@@ -470,20 +481,22 @@
         settle(g_send.at[op, 0 : COLS - SHARE, :], g_s.at[op], g_r.at[op], at_s(1)).wait_send()
         for leg in range(2):
             settle(
-                p_recv.at[op, leg, 0 : OWN - 1], p_s.at[op, leg], p_r.at[op, leg], at_a(1)
+                p_recv.at[op, leg, 0 : OWN - 1, 0 : depth(op)],
+                p_s.at[op, leg], p_r.at[op, leg], at_a(1),
             ).wait_send()
     settle(field.at[1, 0 : COLS - SHARE, :], x_s, x_r, at_s(1)).wait_send()
     settle(norm_recv.at[0 : S - 1], n_s, n_r, at_s(1)).wait_send()
-    for batch in range(2):
-        settle(
-            dot_recv.at[batch, 0 : OWN - 1], d_s.at[batch], d_r.at[batch], at_a(1)
-        ).wait_send()
+
+
+def put_out(x, r, x_out, r_out):
+    x_out[...] = x[...]
+    r_out[...] = r[...]
 
 
 def local(geno, freq, rhs, diag, mend, weight, send_rows, sire, dam):
     vmem = pl.BlockSpec(memory_space=pltpu.VMEM)
     dma = pltpu.SemaphoreType.DMA
-    return pl.pallas_call(
+    results = pl.pallas_call(
         kernel,
         out_shape=(jax.ShapeDtypeStruct((ROWS, COLS), F32),) * 2,
         in_specs=[pl.BlockSpec(memory_space=pl.ANY)] + [vmem] * 8,
@@ -495,8 +508,8 @@
             pltpu.VMEM((2, COLS, ROWS), BF16),
             pltpu.VMEM((COLS, ROWS), F32),
             pltpu.VMEM((COLS, ROWS), F32),
-            pltpu.VMEM((COLS, YCH), F32),
-            pltpu.VMEM((2, Y, COLS, YCH), BF16),
+            pltpu.VMEM((COLS, LOCAL), F32),
+            pltpu.VMEM((2, COLS, LOCAL), BF16),
             pltpu.VMEM((2, Y, COLS, YCH), BF16),
             pltpu.VMEM((COLS, YCH), F32),
             pltpu.VMEM((2, COLS, YCH), BF16),
@@ -505,18 +518,16 @@
             pltpu.VMEM((COLS, ROWS), F32),
             pltpu.VMEM((2, COLS, ROWS), BF16),
             pltpu.VMEM((2, S, SHARE, ROWS), BF16),
-            pltpu.VMEM((2, 2, OWN, SHARE, 2 * SLOTS), BF16),
-            pltpu.VMEM((2, 2, OWN, SHARE, 2 * SLOTS), BF16),
+            pltpu.VMEM((2, 2, OWN, 2 * SHARE, 2 * SLOTS), BF16),
+            pltpu.VMEM((2, 2, OWN, 2 * SHARE, 2 * SLOTS), BF16),
             pltpu.VMEM((2 * SHARE, OWN * SLOTS), BF16),
-            pltpu.VMEM((2, SHARE, 128), F32),
-            pltpu.VMEM((2, OWN, SHARE, 128), F32),
             pltpu.VMEM((COLS, ROWS), F32),
             pltpu.VMEM((COLS, ROWS), BF16),
             pltpu.VMEM((COLS, 128), F32),
             pltpu.VMEM((COLS, 128), F32),
             pltpu.VMEM((COLS, 128), F32),
             pltpu.VMEM((S, SHARE, 128), F32),
-            dma((Y, SUBS)),
+            dma((SUBS,)),
             dma((2, Y - 1, SUBS)), dma((2, Y, SUBS)),
             dma((2, SUBS)), dma((2, SUBS)),
             dma((2, SUBS)), dma((2, SUBS)),
@@ -524,7 +535,6 @@
             dma((2,)), dma((2,)),
             dma, dma,
             dma((2, 2)), dma((2, 2)),
-            dma((2,)), dma((2,)),
             dma, dma,
             dma, dma,
             dma, dma,
@@ -547,6 +557,14 @@
         sire.reshape(1, ROWS),
         dam.reshape(1, ROWS),
     )
+    half = pl.BlockSpec((ROWS // 2, COLS), lambda i: (i, 0))
+    return pl.pallas_call(
+        put_out,
+        grid=(2,),
+        out_shape=(jax.ShapeDtypeStruct((ROWS, COLS), F32),) * 2,
+        in_specs=[half] * 2,
+        out_specs=(half,) * 2,
+    )(*results)
 
 
 def solution(mesh):

time: 120 us -> 113 us (0.942)
  local copies, waits for them, and re-layouts: 3.74 us -> 0 us
  Pallas kernels: 115 us -> 113 us
    pallas_call x1, Pallas kernels: 115 us -> 110 us  [local(): pl.pallas_call(kernel, out_shape=(jax.ShapeDtypeStruct((ROWS, COLS), F32)...]
    unnamed x2 -> x0, local copies, waits for them, and re-layouts: 3.74 us -> none
    pallas_call x0 -> x1, Pallas kernels: none -> 2.04 us  [local(): pl.pallas_call(put_out, grid=(2,), out_shape=(jax.ShapeDtypeStruct((ROWS,...]
where the time goes in v3:
time: 113 us
  Pallas kernels  113 us (100%)
    pallas_call x1, Pallas kernels, local(): pl.pallas_call(kernel, out_shape=(jax.ShapeDtypeStruct((ROWS, COLS), F32)...  110 us

profile of v3, /device:TPU:1, one launch (start us, length us, event | category | flops | bytes accessed | tf_op | source)
XLA Modules:
  0.0 113.1 jit_solution(14377440871461265789)
XLA Ops:
  0.6 110.5 %shard_map.104 = (f32[1024,128]{1,0:T(8,128)}, f32[1024,128]{1,0:T(8,128)}) custom-call(bf16[1024,4096]{1,0:T(8,128)(2,1)} %geno.1, f32[1,4096]{1,0:T(1,128)} %bitcast.6, f32[1024,128]{1,0:T(8,128)} %rhs.1, f32[1024,128]{1,0:T(8,128)} %diag.1, f32[1,1024]{1,0:T(1,128)} %bitcast.8, f32[1,128]{1,0:T(1,128)} %bitcast.11, s32[32,64]{1,0:T(8,128)} %bitcast.7, ...), custom_call_target="tpu_custom_call" | custom-call | flops 5000000000 | bytes 12000000 | tf_op jit(solution)/shard_map/pallas_call | solution.py:499
  111.1 2.0 %shard_map.105 = (f32[1024,128]{1,0:T(8,128)}, f32[1024,128]{1,0:T(8,128)}) custom-call(f32[1024,128]{1,0:T(8,128)} %get-tuple-element.4.x, f32[1024,128]{1,0:T(8,128)} %get-tuple-element.5.r), custom_call_target="tpu_custom_call" | custom-call | tf_op jit(solution)/shard_map/pallas_call | solution.py:561

commit v4 on v3

--- a/solution.py
+++ b/solution.py
@@ -16,6 +16,7 @@
 ZSHARE = COLS // Z
 YCH = LOCAL // Y
 SUBS = 4
+LAST = SUBS - 1
 SUB = YCH // SUBS
 SLOTS = 64
 PARTS = 3
@@ -46,10 +47,11 @@
     x_out, r_out,
     block, send_hot, parent_hot, field, field_t, diag_t,
     y_own, y_send, y_recv, z_own, z_send, z_recv, effects,
-    g_own, g_send, g_recv, p_send, p_recv, p_mat,
-    w_full, result, scalars, norm, norm_send, norm_recv,
+    g_own, g_send, g_recv, p_send, p_half, p_recv, p_mat,
+    w_full, result, scalars, norm, norm_send, norm_recv, turn_recv, turn_own, turn_send, turn_end,
     load_sem, y_s, y_r, z_s, z_r, zg_s, zg_r, yg_s, yg_r, g_s, g_r, x_s, x_r,
     p_s, p_r, w_s, w_r, c_s, c_r, f_s, f_r, n_s, n_r,
+    h_s, h_r, tz_s, tz_r, ty_s, ty_r, tyg_s, tyg_r, tzg_s, tzg_r,
 ):
     a, s = lax.axis_index("animal"), lax.axis_index("snp")
     z, y = a // Y, a % Y
@@ -62,9 +64,6 @@
 
     def at_s(k):
         return (a, (s + k) % S)
-
-    def at_a(k):
-        return ((a + k) % OWN, s)
 
     def remote(src, dst, send_sem, recv_sem, peer):
         return pltpu.make_async_remote_copy(
@@ -91,16 +90,9 @@
 
     barrier = pltpu.get_barrier_semaphore()
 
-    def greet_a(k, carry):
-        pl.semaphore_signal(barrier, inc=1, device_id=at_a(k), device_id_type=MESH)
-        return carry
-
-    def greet_s(k, carry):
-        pl.semaphore_signal(barrier, inc=1, device_id=at_s(k), device_id_type=MESH)
-        return carry
-
-    lax.fori_loop(1, OWN, greet_a, 0)
-    lax.fori_loop(1, S, greet_s, 0)
+    for peers, count in ((at_y, Y), (at_z, Z), (at_s, S)):
+        for k in range(1, count):
+            pl.semaphore_signal(barrier, inc=1, device_id=peers(k), device_id_type=MESH)
 
     field_t[...] = rhs[...].T
     field[0] = field_t[...].astype(BF16)
@@ -183,6 +175,61 @@
 
         lax.fori_loop(1, Z, give, 0)
 
+    def turn_out(op):
+        def give(k, carry):
+            peer_rows = pl.ds(pl.multiple_of(((z + k) % Z) * ZSHARE, ZSHARE), ZSHARE)
+            remote(
+                y_send.at[op, peer_rows, chunk(LAST)], turn_recv.at[op, z],
+                tz_s.at[op], tz_r.at[op], at_z(k),
+            ).start()
+            return carry
+
+        lax.fori_loop(1, Z, give, 0)
+
+    def turn_mid(op):
+        settle(turn_recv.at[op, 0 : Z - 1], tz_s.at[op], tz_r.at[op], at_z(1)).wait_recv()
+        total = y_own[z_mine, chunk(LAST)]
+        for k in range(1, Z):
+            total = total + turn_recv[op, (z + k) % Z].astype(F32)
+        turn_own[...] = total
+        turn_send[op] = total.astype(BF16)
+        for k in range(1, Y):
+            lanes = pl.ds(pl.multiple_of(((y + k) % Y) * SUB, SUB), SUB)
+            remote(
+                turn_send.at[op, :, lanes], turn_end.at[op, y], ty_s.at[op], ty_r.at[op], at_y(k)
+            ).start()
+
+    def turn_sum(op):
+        settle(turn_end.at[op, 0 : Y - 1], ty_s.at[op], ty_r.at[op], at_y(1)).wait_recv()
+        total = turn_own[:, pl.ds(pl.multiple_of(y * SUB, SUB), SUB)]
+        for k in range(1, Y):
+            total = total + turn_end[op, (y + k) % Y].astype(F32)
+        effects[op, z_mine, y_lanes(y, LAST)] = total.astype(BF16)
+        for k in range(1, Y):
+            piece = effects.at[op, z_mine, y_lanes(y, LAST)]
+            remote(piece, piece, tyg_s.at[op], tyg_r.at[op], at_y(k)).start()
+
+    def turn_rows(op):
+        return settle(
+            effects.at[op, 0 : (Y - 1) * ZSHARE, y_lanes(y, LAST)],
+            tyg_s.at[op], tyg_r.at[op], at_y(1),
+        )
+
+    def turn_all(op):
+        return settle(
+            effects.at[op, 0 : COLS - ZSHARE, chunk(LAST)], tzg_s.at[op], tzg_r.at[op], at_z(1)
+        )
+
+    def turn_spread(op):
+        turn_rows(op).wait_recv()
+
+        def give(k, carry):
+            piece = effects.at[op, z_mine, chunk(LAST)]
+            remote(piece, piece, tzg_s.at[op], tzg_r.at[op], at_z(k)).start()
+            return carry
+
+        lax.fori_loop(1, Z, give, 0)
+
     def effects_spread(op, sub):
         lanes = y_lanes(y, sub)
         settle(
@@ -193,7 +240,9 @@
             remote(piece, piece, yg_s.at[op, k - 1, sub], yg_r.at[op, y, sub], at_y(k)).start()
 
     def take(op, sub):
-        for k in range(1, Y):
+        if sub == LAST:
+            turn_all(op).wait_recv()
+        for k in range(1, Y if sub < LAST else 1):
             which = (y + k) % Y
             settle(
                 effects.at[op, :, y_lanes(which, sub)],
@@ -260,8 +309,8 @@
         for pair in range(OWN // 2):
             lanes = slice(pair * 2 * SLOTS, (pair + 1) * 2 * SLOTS)
             high, low = both[:SHARE, lanes], both[SHARE:, lanes]
-            p_send[op, leg, 2 * pair, :SHARE] = jnp.where(first, high, swap(low)).astype(BF16)
-            p_send[op, leg, 2 * pair + 1, :SHARE] = jnp.where(first, swap(high), low).astype(BF16)
+            p_send[op, leg, 2 * pair // Y, 2 * pair % Y, :SHARE] = jnp.where(first, high, swap(low)).astype(BF16)
+            p_send[op, leg, 2 * pair // Y, 2 * pair % Y + 1, :SHARE] = jnp.where(first, swap(high), low).astype(BF16)
         if products:
             parts = []
             for product in products:
@@ -272,24 +321,45 @@
                     parts.append(part)
             tile = pack(*parts).astype(BF16)
             for peer in range(OWN):
-                p_send[op, leg, peer, SHARE:] = tile
-
-        def give(k, carry):
-            peer = (a + k) % OWN
+                p_send[op, leg, peer // Y, peer % Y, SHARE:] = tile
+
+    def relay_y(leg, op):
+        return settle(
+            p_half.at[op, leg, 0 : Y - 1, :, 0 : depth(op)],
+            p_s.at[op, leg], p_r.at[op, leg], at_y(1),
+        )
+
+    def relay_z(leg, op):
+        return settle(
+            p_recv.at[op, leg, 0 : OWN - Y, 0 : depth(op)], h_s.at[op, leg], h_r.at[op, leg], at_z(1)
+        )
+
+    def relay_send(leg, op):
+        for k in range(1, Y):
             remote(
-                p_send.at[op, leg, peer, 0 : depth(op)], p_recv.at[op, leg, a, 0 : depth(op)],
-                p_s.at[op, leg], p_r.at[op, leg], at_a(k),
+                p_send.at[op, leg, :, (y + k) % Y, 0 : depth(op)],
+                p_half.at[op, leg, y, :, 0 : depth(op)],
+                p_s.at[op, leg], p_r.at[op, leg], at_y(k),
             ).start()
-            return carry
-
-        lax.fori_loop(1, OWN, give, 0)
+        p_half[op, leg, y, :, : depth(op)] = p_send[op, leg, :, y, : depth(op)]
+
+    def relay_turn(leg, op):
+        relay_y(leg, op).wait_recv()
+        own = pl.ds(z * Y, Y)
+
+        def give(k, carry):
+            remote(
+                p_half.at[op, leg, :, (z + k) % Z, 0 : depth(op)],
+                p_recv.at[op, leg, own, 0 : depth(op)],
+                h_s.at[op, leg], h_r.at[op, leg], at_z(k),
+            ).start()
+            return carry
+
+        lax.fori_loop(1, Z, give, 0)
+        p_recv[op, leg, own, : depth(op)] = p_half[op, leg, :, z, : depth(op)]
 
     def relay_in(leg, op):
-        settle(
-            p_recv.at[op, leg, 0 : OWN - 1, 0 : depth(op)],
-            p_s.at[op, leg], p_r.at[op, leg], at_a(1),
-        ).wait_recv()
-        p_recv[op, leg, a] = p_send[op, leg, a]
+        relay_z(leg, op).wait_recv()
         for pair in range(OWN // 2):
             lanes = slice(pair * 2 * SLOTS, (pair + 1) * 2 * SLOTS)
             one = p_recv[op, leg, 2 * pair, :SHARE].astype(F32)
@@ -339,6 +409,7 @@
         both = jnp.concatenate([high, back - high], axis=0)
         if op == 0:
             relay_out(1, op, both)
+            relay_send(1, op)
             return ()
         gamma, delta, square = totals(0)
         alpha = gamma / delta
@@ -346,6 +417,7 @@
         relay_out(
             1, op, both, (rest * rest, rest * value, d_share * value * value + term * lacks)
         )
+        relay_send(1, op)
         return gamma, alpha, square, rest
 
     def pedigree_end(op, term):
@@ -375,72 +447,80 @@
     def all_of(ref, send_sem, recv_sem):
         return settle(ref.at[0 : COLS - SHARE, :], send_sem, recv_sem, at_s(1))
 
-    effects_out(0, 0, send=False)
-    effects_out(0, 1, send=False)
+    for sub in range(SUBS):
+        effects_out(0, sub, send=False)
     make_send_hot()
-    pl.semaphore_wait(barrier, OWN - 1 + S - 1)
+    pedigree_out(0, b_share)
+    pl.semaphore_wait(barrier, Y - 1 + Z - 1 + S - 1)
+    turn_out(0)
     effects_send(0, 0)
+    relay_send(0, 0)
     effects_send(0, 1)
-    effects_out(0, 2)
-    effects_out(0, 3)
-    pedigree_out(0, b_share)
     make_parent_hot()
     diag_t[...] = diag[...].T
     d_share = diag_t[mine, :]
     effects_mid(0, 0)
+    effects_send(0, 2)
+    relay_turn(0, 0)
     effects_mid(0, 1)
+    turn_mid(0)
     effects_mid(0, 2)
     effects_sum(0, 0)
-    effects_mid(0, 3)
     effects_sum(0, 1)
+    turn_sum(0)
     lacks, term = pedigree_mid(0, b_share)
     effects_spread(0, 0)
+    effects_sum(0, 2)
+    turn_spread(0)
     pedigree_back(0, b_share, lacks, term)
-    effects_sum(0, 2)
     effects_spread(0, 1)
-    effects_sum(0, 3)
     effects_spread(0, 2)
+    relay_turn(1, 0)
     take(0, 0)
-    effects_spread(0, 3)
     take(0, 1)
     take(0, 2)
-    ped = pedigree_end(0, term)
     take(0, 3)
     genomic_out(0)
+    ped = pedigree_end(0, term)
     w_share = d_share * b_share + ped
     w_share = w_share + scale * genomic_in(0)
     share_field(w_share)
     pedigree_out(1, w_share, (b_share * b_share, w_share * b_share, w_share * w_share))
+    relay_send(0, 1)
     w_full[mine, :] = w_share
     field_arrives()
 
+    effects_out(1, 3, send=False)
+    turn_out(1)
     effects_out(1, 0)
     effects_out(1, 1)
-    effects_out(1, 2)
-    effects_out(1, 3)
+    effects_out(1, 2, send=False)
+    relay_turn(0, 1)
+    effects_mid(1, 0)
+    effects_send(1, 2)
     to_snp(w_full, w_s, w_r)
+    effects_mid(1, 1)
     lacks, term = pedigree_mid(1, w_share)
-    effects_mid(1, 0)
-    gamma0, alpha0, square0, r_share = pedigree_back(1, w_share, lacks, term)
-    effects_mid(1, 1)
+    turn_mid(1)
     effects_mid(1, 2)
     effects_sum(1, 0)
-    effects_mid(1, 3)
     effects_sum(1, 1)
+    turn_sum(1)
+    gamma0, alpha0, square0, r_share = pedigree_back(1, w_share, lacks, term)
     effects_spread(1, 0)
     effects_sum(1, 2)
+    turn_spread(1)
     effects_spread(1, 1)
-    effects_sum(1, 3)
-    ped = pedigree_end(1, term)
+    relay_turn(1, 1)
     effects_spread(1, 2)
     take(1, 0)
-    effects_spread(1, 3)
     take(1, 1)
     take(1, 2)
+    take(1, 3)
+    genomic_out(1)
+    ped = pedigree_end(1, term)
     gamma1, cross, quad = totals(1)
     beta = gamma1 / gamma0
-    take(1, 3)
-    genomic_out(1)
     quad = quad + scale * norm_in()
     delta1 = cross - alpha0 * (square0 - alpha0 * quad)
     alpha1 = gamma1 / (delta1 - beta * gamma1 / alpha0)
@@ -461,7 +541,11 @@
     r_out[...] = result[...].astype(F32).T
 
     for op in range(2):
-        for sub in range(SUBS):
+        settle(turn_recv.at[op, 0 : Z - 1], tz_s.at[op], tz_r.at[op], at_z(1)).wait_send()
+        settle(turn_end.at[op, 0 : Y - 1], ty_s.at[op], ty_r.at[op], at_y(1)).wait_send()
+        turn_rows(op).wait_send()
+        turn_all(op).wait_send()
+        for sub in range(LAST):
             here = spot(sub)
             for k in range(1, Y):
                 settle(
@@ -480,10 +564,8 @@
             ).wait_send()
         settle(g_send.at[op, 0 : COLS - SHARE, :], g_s.at[op], g_r.at[op], at_s(1)).wait_send()
         for leg in range(2):
-            settle(
-                p_recv.at[op, leg, 0 : OWN - 1, 0 : depth(op)],
-                p_s.at[op, leg], p_r.at[op, leg], at_a(1),
-            ).wait_send()
+            relay_y(leg, op).wait_send()
+            relay_z(leg, op).wait_send()
     settle(field.at[1, 0 : COLS - SHARE, :], x_s, x_r, at_s(1)).wait_send()
     settle(norm_recv.at[0 : S - 1], n_s, n_r, at_s(1)).wait_send()
 
@@ -518,7 +600,8 @@
             pltpu.VMEM((COLS, ROWS), F32),
             pltpu.VMEM((2, COLS, ROWS), BF16),
             pltpu.VMEM((2, S, SHARE, ROWS), BF16),
-            pltpu.VMEM((2, 2, OWN, 2 * SHARE, 2 * SLOTS), BF16),
+            pltpu.VMEM((2, 2, Z, Y, 2 * SHARE, 2 * SLOTS), BF16),
+            pltpu.VMEM((2, 2, Y, Z, 2 * SHARE, 2 * SLOTS), BF16),
             pltpu.VMEM((2, 2, OWN, 2 * SHARE, 2 * SLOTS), BF16),
             pltpu.VMEM((2 * SHARE, OWN * SLOTS), BF16),
             pltpu.VMEM((COLS, ROWS), F32),
@@ -527,6 +610,10 @@
             pltpu.VMEM((COLS, 128), F32),
             pltpu.VMEM((COLS, 128), F32),
             pltpu.VMEM((S, SHARE, 128), F32),
+            pltpu.VMEM((2, Z, ZSHARE, YCH), BF16),
+            pltpu.VMEM((ZSHARE, YCH), F32),
+            pltpu.VMEM((2, ZSHARE, YCH), BF16),
+            pltpu.VMEM((2, Y, ZSHARE, SUB), BF16),
             dma((SUBS,)),
             dma((2, Y - 1, SUBS)), dma((2, Y, SUBS)),
             dma((2, SUBS)), dma((2, SUBS)),
@@ -539,6 +626,8 @@
             dma, dma,
             dma, dma,
             dma, dma,
+            dma((2, 2)), dma((2, 2)),
+            *[dma((2,))] * 8,
         ],
         compiler_params=pltpu.CompilerParams(
             collective_id=0, has_side_effects=True, vmem_limit_bytes=56 * 2**20

time: 113 us -> 109 us (0.965)
  Pallas kernels: 113 us -> 108 us
    pallas_call x1, Pallas kernels: 110 us -> 106 us  [local(): pl.pallas_call(kernel, out_shape=(jax.ShapeDtypeStruct((ROWS, COLS), F32)...]
where the time goes in v4:
time: 109 us
  Pallas kernels  108 us (99%)
    pallas_call x1, Pallas kernels, local(): pl.pallas_call(kernel, out_shape=(jax.ShapeDtypeStruct((ROWS, COLS), F32)...  106 us

profile of v4, /device:TPU:1, one launch (start us, length us, event | category | flops | bytes accessed | tf_op | source)
XLA Modules:
  0.0 108.6 jit_solution(12788646426370111826)
XLA Ops:
  0.6 105.9 %shard_map.104 = (f32[1024,128]{1,0:T(8,128)}, f32[1024,128]{1,0:T(8,128)}) custom-call(bf16[1024,4096]{1,0:T(8,128)(2,1)} %geno.1, f32[1,4096]{1,0:T(1,128)} %bitcast.6, f32[1024,128]{1,0:T(8,128)} %rhs.1, f32[1024,128]{1,0:T(8,128)} %diag.1, f32[1,1024]{1,0:T(1,128)} %bitcast.8, f32[1,128]{1,0:T(1,128)} %bitcast.11, s32[32,64]{1,0:T(8,128)} %bitcast.7, ...), custom_call_target="tpu_custom_call" | custom-call | flops 5000000000 | bytes 12000000 | tf_op jit(solution)/shard_map/pallas_call | solution.py:581
  106.6 2.0 %shard_map.105 = (f32[1024,128]{1,0:T(8,128)}, f32[1024,128]{1,0:T(8,128)}) custom-call(f32[1024,128]{1,0:T(8,128)} %get-tuple-element.4.x, f32[1024,128]{1,0:T(8,128)} %get-tuple-element.5.r), custom_call_target="tpu_custom_call" | custom-call | tf_op jit(solution)/shard_map/pallas_call | solution.py:650

commit v5 on v4

--- a/solution.py
+++ b/solution.py
@@ -47,7 +47,7 @@
     x_out, r_out,
     block, send_hot, parent_hot, field, field_t, diag_t,
     y_own, y_send, y_recv, z_own, z_send, z_recv, effects,
-    g_own, g_send, g_recv, p_send, p_half, p_recv, p_mat,
+    g_own, g_send, g_recv, y_box, z_box, p_mat,
     w_full, result, scalars, norm, norm_send, norm_recv, turn_recv, turn_own, turn_send, turn_end,
     load_sem, y_s, y_r, z_s, z_r, zg_s, zg_r, yg_s, yg_r, g_s, g_r, x_s, x_r,
     p_s, p_r, w_s, w_r, c_s, c_r, f_s, f_r, n_s, n_r,
@@ -302,89 +302,151 @@
             tile = jnp.where(lane == position, column, tile)
         return tile
 
-    def depth(op):
-        return 2 * SHARE if op == 1 else SHARE
-
-    def relay_out(leg, op, both, products=()):
-        for pair in range(OWN // 2):
-            lanes = slice(pair * 2 * SLOTS, (pair + 1) * 2 * SLOTS)
-            high, low = both[:SHARE, lanes], both[SHARE:, lanes]
-            p_send[op, leg, 2 * pair // Y, 2 * pair % Y, :SHARE] = jnp.where(first, high, swap(low)).astype(BF16)
-            p_send[op, leg, 2 * pair // Y, 2 * pair % Y + 1, :SHARE] = jnp.where(first, swap(high), low).astype(BF16)
-        if products:
-            parts = []
-            for product in products:
-                left = jnp.sum(product, axis=1, keepdims=True)
-                for _ in range(PARTS):
-                    part = left.astype(BF16).astype(F32)
-                    left = left - part
-                    parts.append(part)
-            tile = pack(*parts).astype(BF16)
-            for peer in range(OWN):
-                p_send[op, leg, peer // Y, peer % Y, SHARE:] = tile
-
-    def relay_y(leg, op):
+    def in_y(op):
+        return Z + 1 if op == 1 else Z
+
+    def in_z(op):
+        return Y + 1 if op == 1 else Y
+
+    def split(columns):
+        parts = []
+        for left in columns:
+            for _ in range(PARTS):
+                part = left.astype(BF16).astype(F32)
+                left = left - part
+                parts.append(part)
+        return pack(*parts).astype(BF16)
+
+    def column_sums(products):
+        return [jnp.sum(p, axis=1, keepdims=True) for p in products]
+
+    def joined(tiles):
+        tile = jnp.sum(tiles.astype(F32), axis=0)
+        return tuple(
+            jnp.sum(tile[:, i * PARTS : (i + 1) * PARTS], axis=1, keepdims=True) for i in range(3)
+        )
+
+    def y_waits(leg, op):
         return settle(
-            p_half.at[op, leg, 0 : Y - 1, :, 0 : depth(op)],
+            y_box.at[op, 2 * leg + 1, 0 : Y - 1, 0 : in_y(op)],
             p_s.at[op, leg], p_r.at[op, leg], at_y(1),
         )
 
-    def relay_z(leg, op):
+    def z_waits(leg, op):
         return settle(
-            p_recv.at[op, leg, 0 : OWN - Y, 0 : depth(op)], h_s.at[op, leg], h_r.at[op, leg], at_z(1)
-        )
-
-    def relay_send(leg, op):
+            z_box.at[op, 2 * leg + 1, 0 : Z - 1, 0 : in_z(op)],
+            h_s.at[op, leg], h_r.at[op, leg], at_z(1),
+        )
+
+    def along_y(leg, op):
+        size = in_y(op)
         for k in range(1, Y):
             remote(
-                p_send.at[op, leg, :, (y + k) % Y, 0 : depth(op)],
-                p_half.at[op, leg, y, :, 0 : depth(op)],
+                y_box.at[op, 2 * leg, (y + k) % Y, 0:size],
+                y_box.at[op, 2 * leg + 1, y, 0:size],
                 p_s.at[op, leg], p_r.at[op, leg], at_y(k),
             ).start()
-        p_half[op, leg, y, :, : depth(op)] = p_send[op, leg, :, y, : depth(op)]
-
-    def relay_turn(leg, op):
-        relay_y(leg, op).wait_recv()
-        own = pl.ds(z * Y, Y)
+        y_box[op, 2 * leg + 1, y, :size] = y_box[op, 2 * leg, y, :size]
+
+    def along_z(leg, op):
+        size = in_z(op)
 
         def give(k, carry):
             remote(
-                p_half.at[op, leg, :, (z + k) % Z, 0 : depth(op)],
-                p_recv.at[op, leg, own, 0 : depth(op)],
+                z_box.at[op, 2 * leg, (z + k) % Z, 0:size],
+                z_box.at[op, 2 * leg + 1, z, 0:size],
                 h_s.at[op, leg], h_r.at[op, leg], at_z(k),
             ).start()
             return carry
 
         lax.fori_loop(1, Z, give, 0)
-        p_recv[op, leg, own, : depth(op)] = p_half[op, leg, :, z, : depth(op)]
-
-    def relay_in(leg, op):
-        relay_z(leg, op).wait_recv()
-        for pair in range(OWN // 2):
-            lanes = slice(pair * 2 * SLOTS, (pair + 1) * 2 * SLOTS)
-            one = p_recv[op, leg, 2 * pair, :SHARE].astype(F32)
-            two = p_recv[op, leg, 2 * pair + 1, :SHARE].astype(F32)
-            p_mat[:SHARE, lanes] = jnp.where(first, one, swap(two)).astype(BF16)
-            p_mat[SHARE:, lanes] = jnp.where(first, swap(one), two).astype(BF16)
+        z_box[op, 2 * leg + 1, z, :size] = z_box[op, 2 * leg, z, :size]
+
+    def regroup(one, two):
+        one, two = one.astype(F32), two.astype(F32)
+        return (
+            jnp.where(first, one, swap(two)).astype(BF16),
+            jnp.where(first, swap(one), two).astype(BF16),
+        )
+
+    def relay_out(op, tiles, products=()):
+        for i in range(OWN // 2):
+            lanes = slice(i * 128, (i + 1) * 128)
+            y_box[op, 0, i // 4, i % 4] = tiles[:SHARE, lanes].astype(BF16)
+            y_box[op, 0, i // 4, 4 + i % 4] = tiles[SHARE:, lanes].astype(BF16)
+        if products:
+            tile = split(column_sums(products))
+            for peer in range(Y):
+                y_box[op, 0, peer, Z] = tile
+
+    def relay_turn(op):
+        y_waits(0, op).wait_recv()
+        for m in range(Z // 2):
+            for pair, part in ((0, 0), (1, 0), (0, 1), (1, 1)):
+                at = 4 * part + m
+                one, two = regroup(y_box[op, 1, 2 * pair, at], y_box[op, 1, 2 * pair + 1, at])
+                z_box[op, 0, 2 * m, 2 * part + pair] = one
+                z_box[op, 0, 2 * m + 1, 2 * part + pair] = two
+        if op == 1:
+            tile = split(joined(y_box[1, 1, :, Z]))
+            for peer in range(Z):
+                z_box[1, 0, peer, Y] = tile
+        along_z(0, op)
+
+    def relay_in(op):
+        z_waits(0, op).wait_recv()
+        for i in range(OWN // 2):
+            lanes = slice(i * 128, (i + 1) * 128)
+            p_mat[:SHARE, lanes] = z_box[op, 1, i // 2, i % 2]
+            p_mat[SHARE:, lanes] = z_box[op, 1, i // 2, 2 + i % 2]
         return p_mat[...]
 
-    def totals(leg):
-        tile = jnp.sum(p_recv[1, leg, :, SHARE:, :].astype(F32), axis=0)
-        return tuple(
-            jnp.sum(tile[:, i * PARTS : (i + 1) * PARTS], axis=1, keepdims=True) for i in range(3)
-        )
+    def return_out(op, tiles, products=()):
+        for i in range(OWN // 2):
+            tile = tiles[:, i * 128 : (i + 1) * 128]
+            high = tile.astype(BF16)
+            z_box[op, 2, i // 2, i % 2] = high
+            z_box[op, 2, i // 2, 2 + i % 2] = (tile - high.astype(F32)).astype(BF16)
+        if products:
+            tile = split(column_sums(products))
+            for peer in range(Z):
+                z_box[op, 2, peer, Y] = tile
+        along_z(1, op)
+
+    def return_turn(op):
+        z_waits(1, op).wait_recv()
+        for m in range(Z // 2):
+            for pair, part in ((0, 0), (1, 0), (0, 1), (1, 1)):
+                at = 2 * part + pair
+                one, two = regroup(z_box[op, 3, 2 * m, at], z_box[op, 3, 2 * m + 1, at])
+                y_box[op, 2, 2 * pair, 4 * part + m] = one
+                y_box[op, 2, 2 * pair + 1, 4 * part + m] = two
+        if op == 1:
+            tile = split(joined(z_box[1, 3, :, Y]))
+            for peer in range(Y):
+                y_box[1, 2, peer, Z] = tile
+        along_y(1, op)
+
+    def return_in(op):
+        y_waits(1, op).wait_recv()
+        for i in range(OWN // 2):
+            lanes = slice(i * 128, (i + 1) * 128)
+            p_mat[:SHARE, lanes] = y_box[op, 3, i // 4, i % 4]
+            p_mat[SHARE:, lanes] = y_box[op, 3, i // 4, 4 + i % 4]
+        return p_mat[...]
 
     def fold(both):
         return both[:SHARE] + both[SHARE:]
 
     def make_send_hot():
-        even = rows[pl.ds(0, OWN // 2, stride=2), :]
-        odd = rows[pl.ds(1, OWN // 2, stride=2), :]
-        pairs = jnp.concatenate([even, odd], axis=1)
         at = lax.broadcasted_iota(jnp.int32, (ROWS, 2 * SLOTS), 0)
-        for pair in range(OWN // 2):
-            lanes = slice(pair * 2 * SLOTS, (pair + 1) * 2 * SLOTS)
-            send_hot[:, lanes] = (at == pairs[pair : pair + 1, :]).astype(F32).astype(BF16)
+        for peer in range(Y):
+            even = rows[pl.ds(peer, Z // 2, stride=2 * Y), :]
+            odd = rows[pl.ds(peer + Y, Z // 2, stride=2 * Y), :]
+            pairs = jnp.concatenate([even, odd], axis=1)
+            for m in range(Z // 2):
+                lanes = slice((peer * 4 + m) * 128, (peer * 4 + m + 1) * 128)
+                send_hot[:, lanes] = (at == pairs[m : m + 1, :]).astype(F32).astype(BF16)
 
     def make_parent_hot():
         def some(i, carry):
@@ -396,32 +458,28 @@
         lax.fori_loop(0, OWN * SLOTS // 128, some, 0)
 
     def pedigree_out(op, value, products=()):
-        relay_out(0, op, dot(halves(value), send_hot[...]), products)
+        relay_out(op, dot(halves(value), send_hot[...]), products)
 
     def pedigree_mid(op, value):
-        parents = fold(dot(relay_in(0, op), parent_hot[...]))
+        parents = fold(dot(relay_in(op), parent_hot[...]))
         lacks = value - 0.5 * parents
         return lacks, mend[...] * lacks
 
     def pedigree_back(op, value, lacks, term):
         back = -0.5 * fold(dot_nt(halves(term), parent_hot[...]))
-        high = back.astype(BF16).astype(F32)
-        both = jnp.concatenate([high, back - high], axis=0)
         if op == 0:
-            relay_out(1, op, both)
-            relay_send(1, op)
+            return_out(op, back)
             return ()
-        gamma, delta, square = totals(0)
+        gamma, delta, square = joined(z_box[1, 1, :, Y])
         alpha = gamma / delta
         rest = b_share - alpha * value
-        relay_out(
-            1, op, both, (rest * rest, rest * value, d_share * value * value + term * lacks)
-        )
-        relay_send(1, op)
+        return_out(
+            op, back, (rest * rest, rest * value, d_share * value * value + term * lacks)
+        )
         return gamma, alpha, square, rest
 
     def pedigree_end(op, term):
-        return term + fold(dot_nt(relay_in(1, op), send_hot[...]))
+        return term + fold(dot_nt(return_in(op), send_hot[...]))
 
     def share_field(value):
         field[1, mine, :] = value.astype(BF16)
@@ -454,28 +512,28 @@
     pl.semaphore_wait(barrier, Y - 1 + Z - 1 + S - 1)
     turn_out(0)
     effects_send(0, 0)
-    relay_send(0, 0)
+    along_y(0, 0)
     effects_send(0, 1)
     make_parent_hot()
     diag_t[...] = diag[...].T
     d_share = diag_t[mine, :]
     effects_mid(0, 0)
     effects_send(0, 2)
-    relay_turn(0, 0)
+    relay_turn(0)
     effects_mid(0, 1)
     turn_mid(0)
     effects_mid(0, 2)
     effects_sum(0, 0)
+    lacks, term = pedigree_mid(0, b_share)
     effects_sum(0, 1)
     turn_sum(0)
-    lacks, term = pedigree_mid(0, b_share)
+    pedigree_back(0, b_share, lacks, term)
     effects_spread(0, 0)
     effects_sum(0, 2)
     turn_spread(0)
-    pedigree_back(0, b_share, lacks, term)
     effects_spread(0, 1)
+    return_turn(0)
     effects_spread(0, 2)
-    relay_turn(1, 0)
     take(0, 0)
     take(0, 1)
     take(0, 2)
@@ -486,7 +544,7 @@
     w_share = w_share + scale * genomic_in(0)
     share_field(w_share)
     pedigree_out(1, w_share, (b_share * b_share, w_share * b_share, w_share * w_share))
-    relay_send(0, 1)
+    along_y(0, 1)
     w_full[mine, :] = w_share
     field_arrives()
 
@@ -495,7 +553,7 @@
     effects_out(1, 0)
     effects_out(1, 1)
     effects_out(1, 2, send=False)
-    relay_turn(0, 1)
+    relay_turn(1)
     effects_mid(1, 0)
     effects_send(1, 2)
     to_snp(w_full, w_s, w_r)
@@ -504,14 +562,14 @@
     turn_mid(1)
     effects_mid(1, 2)
     effects_sum(1, 0)
+    gamma0, alpha0, square0, r_share = pedigree_back(1, w_share, lacks, term)
     effects_sum(1, 1)
     turn_sum(1)
-    gamma0, alpha0, square0, r_share = pedigree_back(1, w_share, lacks, term)
     effects_spread(1, 0)
     effects_sum(1, 2)
     turn_spread(1)
+    return_turn(1)
     effects_spread(1, 1)
-    relay_turn(1, 1)
     effects_spread(1, 2)
     take(1, 0)
     take(1, 1)
@@ -519,7 +577,7 @@
     take(1, 3)
     genomic_out(1)
     ped = pedigree_end(1, term)
-    gamma1, cross, quad = totals(1)
+    gamma1, cross, quad = joined(y_box[1, 3, :, Z])
     beta = gamma1 / gamma0
     quad = quad + scale * norm_in()
     delta1 = cross - alpha0 * (square0 - alpha0 * quad)
@@ -564,8 +622,8 @@
             ).wait_send()
         settle(g_send.at[op, 0 : COLS - SHARE, :], g_s.at[op], g_r.at[op], at_s(1)).wait_send()
         for leg in range(2):
-            relay_y(leg, op).wait_send()
-            relay_z(leg, op).wait_send()
+            y_waits(leg, op).wait_send()
+            z_waits(leg, op).wait_send()
     settle(field.at[1, 0 : COLS - SHARE, :], x_s, x_r, at_s(1)).wait_send()
     settle(norm_recv.at[0 : S - 1], n_s, n_r, at_s(1)).wait_send()
 
@@ -600,9 +658,8 @@
             pltpu.VMEM((COLS, ROWS), F32),
             pltpu.VMEM((2, COLS, ROWS), BF16),
             pltpu.VMEM((2, S, SHARE, ROWS), BF16),
-            pltpu.VMEM((2, 2, Z, Y, 2 * SHARE, 2 * SLOTS), BF16),
-            pltpu.VMEM((2, 2, Y, Z, 2 * SHARE, 2 * SLOTS), BF16),
-            pltpu.VMEM((2, 2, OWN, 2 * SHARE, 2 * SLOTS), BF16),
+            pltpu.VMEM((2, 4, Y, Z + 1, SHARE, 2 * SLOTS), BF16),
+            pltpu.VMEM((2, 4, Z, Y + 1, SHARE, 2 * SLOTS), BF16),
             pltpu.VMEM((2 * SHARE, OWN * SLOTS), BF16),
             pltpu.VMEM((COLS, ROWS), F32),
             pltpu.VMEM((COLS, ROWS), BF16),

time: 109 us -> 108 us (level)
  no operation moved by 1% of the time
where the time goes in v5:
time: 108 us
  Pallas kernels  107 us (99%)
    pallas_call x1, Pallas kernels, local(): pl.pallas_call(kernel, out_shape=(jax.ShapeDtypeStruct((ROWS, COLS), F32)...  105 us

profile of v5, /device:TPU:1, one launch (start us, length us, event | category | flops | bytes accessed | tf_op | source)
XLA Modules:
  0.0 108.1 jit_solution(1082285477317744882)
XLA Ops:
  0.6 105.4 %shard_map.104 = (f32[1024,128]{1,0:T(8,128)}, f32[1024,128]{1,0:T(8,128)}) custom-call(bf16[1024,4096]{1,0:T(8,128)(2,1)} %geno.1, f32[1,4096]{1,0:T(1,128)} %bitcast.6, f32[1024,128]{1,0:T(8,128)} %rhs.1, f32[1024,128]{1,0:T(8,128)} %diag.1, f32[1,1024]{1,0:T(1,128)} %bitcast.8, f32[1,128]{1,0:T(1,128)} %bitcast.11, s32[32,64]{1,0:T(8,128)} %bitcast.7, ...), custom_call_target="tpu_custom_call" | custom-call | flops 5000000000 | bytes 12000000 | tf_op jit(solution)/shard_map/pallas_call | solution.py:639
  106.0 2.0 %shard_map.105 = (f32[1024,128]{1,0:T(8,128)}, f32[1024,128]{1,0:T(8,128)}) custom-call(f32[1024,128]{1,0:T(8,128)} %get-tuple-element.4.x, f32[1024,128]{1,0:T(8,128)} %get-tuple-element.5.r), custom_call_target="tpu_custom_call" | custom-call | tf_op jit(solution)/shard_map/pallas_call | solution.py:707
